TPU v7x, 1024 devices: a whole 4x4x32 slice. The times are simulated.
1024 devices in a mesh: region: 32 (over x, y, core), span: 32 (over z).
Axes of the slice: x: 4, y: 4, z: 32, core: 2. Of those that a mesh axis runs over, the one named last changes fastest.
Arguments:
- column_state: bfloat16 [65536, 288], P(('region', 'span')), may hold values from -5 to 5
- crm_fields: bfloat16 [65536, 5568], P(('region', 'span')), may hold values from -5 to 5
- span_map: int32 [65536], P(('region', 'span')), may hold values from 0 to 31, as said below
- active: int32 [65536], P(('region', 'span')), may hold values from 0 to 1
- density: float32 [58], replicated, may hold values from 0.3 to 1
- nbr_elem: int32 [16384, 4], P(('region', 'span')), may hold values from 0 to 16383, as said below
- nbr_side: int32 [16384, 4], P(('region', 'span')), may hold values from 0 to 3
Outputs:
- column_tendency: bfloat16 [65536, 288], P(('region', 'span'))
- crm_next: bfloat16 [65536, 5568], P(('region', 'span'))
- span_precip: float32 [24576], P(('region', 'span'))
- edge_sums: float32 [16384, 4, 288], P(('region', 'span'))
Inputs may be any that keep to these rules, and one draw needn't show every extreme that they name: `span_map`: among the active columns of one device at most 2 name the same span, and the devices of a region send at most 24 active columns to one span; both bounds are reached in every draw. `nbr_elem`: the neighbour across a side of element e lies within 8 of e in the element order wrapped at 16384, never e itself; distance 8 occurs in both directions.
All inputs are finite; a program needn't handle non-finite values.
Results may differ from a plain program's by a relative error of at most 0.0035.
Values may be sent and summed in bfloat16 or wider, within the bound.
A program may use at most 64 MiB of HBM per device.

v0:
```python
import jax
import jax.numpy as jnp
from jax import lax
from jax.sharding import PartitionSpec as P

HIGH = lax.Precision.HIGHEST


def padded_2(cells, sides, width):
    for axis, dim in sides:
        count = lax.axis_size(axis)
        head = lax.slice_in_dim(cells, 0, width, axis=dim)
        tail = lax.slice_in_dim(cells, cells.shape[dim] - width, cells.shape[dim], axis=dim)
        cells = jnp.concatenate(
            [
                lax.ppermute(tail, axis, [(i, (i + 1) % count) for i in range(count)]),
                cells,
                lax.ppermute(head, axis, [((i + 1) % count, i) for i in range(count)]),
            ],
            axis=dim,
        )
    return cells


def level_map(count_to, count_from):
    indices = jnp.arange(count_to, dtype=jnp.int32)
    numerator = (2 * indices + 1) * count_from - count_to
    denominator = 2 * count_to
    lower_index = jnp.clip(numerator // denominator, 0, count_from - 2)
    fraction = jnp.clip(
        (numerator - lower_index * denominator).astype(jnp.float32) / denominator, 0.0, 1.0
    )
    targets = jnp.arange(count_from, dtype=jnp.int32)[None, :]
    return (1.0 - fraction)[:, None] * (targets == lower_index[:, None]) + fraction[:, None] * (
        targets == lower_index[:, None] + 1
    )


def make_tables(density, levels, height, crm_width):
    up_map = level_map(height, levels)
    down_map = level_map(levels, height)
    midpoint = crm_width // 2
    modes = jnp.arange(crm_width, dtype=jnp.int32)
    wavenumber = jnp.where(modes <= midpoint, modes, modes - midpoint)
    points = jnp.arange(crm_width, dtype=jnp.int32)
    phases = (
        2.0
        * jnp.pi
        * (wavenumber[:, None] * points[None, :] % crm_width).astype(jnp.float32)
        / crm_width
    )
    norms = jnp.where(
        (modes == 0) | (modes == midpoint), jnp.sqrt(1.0 / crm_width), jnp.sqrt(2.0 / crm_width)
    )
    fourier = norms[:, None] * jnp.where(
        (modes <= midpoint)[:, None], jnp.cos(phases), jnp.sin(phases)
    )
    eigenvalue = 2.0 - 2.0 * jnp.cos(2.0 * jnp.pi * wavenumber.astype(jnp.float32) / crm_width)
    faces = 0.5 * (density[1:] + density[:-1])
    upper_face = jnp.concatenate([faces, density[-1:]])
    lower_face = jnp.concatenate([density[:1], faces])
    empty = jnp.zeros((1,), density.dtype)
    main_diag = -eigenvalue[:, None] - ((upper_face + lower_face) / density)[None, :]
    upper_diag = jnp.broadcast_to(
        jnp.concatenate([faces / density[:-1], empty])[None, :], main_diag.shape
    )
    lower_diag = jnp.broadcast_to(
        jnp.concatenate([empty, faces / density[1:]])[None, :], main_diag.shape
    )
    return (up_map, down_map, fourier, lower_diag, main_diag, upper_diag, density)


def diff_x(field):
    return 0.5 * (jnp.roll(field, -1, 2) - jnp.roll(field, 1, 2))


def diff_z(field):
    padded = jnp.pad(field, ((0, 0), (1, 1), (0, 0)))
    return 0.5 * (padded[:, 2:] - padded[:, :-2])


def crm_step(gcm_state, fields, tables, levels, height, crm_width):
    up_map, down_map, fourier, lower_diag, main_diag, upper_diag, density = tables
    column_count = gcm_state.shape[0]
    gcm = gcm_state.astype(jnp.float32).reshape(column_count, 4, levels)
    vertical_profile = jnp.einsum("nfl,kl->nfk", gcm, up_map, precision=HIGH)
    crm_state = fields.astype(jnp.float32).reshape(column_count, 3, height, crm_width)
    wind_x, wind_z, water = (crm_state[:, 0], crm_state[:, 1], crm_state[:, 2])
    force_u = vertical_profile[:, 2] - jnp.mean(wind_x, 2)
    force_q = vertical_profile[:, 1] + vertical_profile[:, 3] - jnp.mean(water, 2)
    buoyant = 0.5 * (water - jnp.mean(water, 2, keepdims=True))
    wind_x1 = (
        wind_x
        - 0.25 * (wind_x * diff_x(wind_x) + wind_z * diff_z(wind_x))
        + 0.25 * force_u[:, :, None]
    )
    wind_z1 = wind_z - 0.25 * (wind_x * diff_x(wind_z) + wind_z * diff_z(wind_z)) + 0.25 * buoyant
    water1 = (
        water
        - 0.25 * (wind_x * diff_x(water) + wind_z * diff_z(water))
        + 0.25 * force_q[:, :, None]
    )
    rho_cells = density[None, :, None]
    divergence = diff_x(wind_x1) + diff_z(rho_cells * wind_z1) / rho_cells
    spectrum = jnp.einsum("nzx,mx->mzn", divergence, fourier, precision=HIGH)
    solved = lax.linalg.tridiagonal_solve(lower_diag, main_diag, upper_diag, spectrum)
    pressure = jnp.einsum("mzn,mx->nzx", solved, fourier, precision=HIGH)
    wind_x2 = wind_x1 - diff_x(pressure)
    wind_z2 = wind_z1 - diff_z(pressure)
    condensate = jax.nn.softplus(water1 - jnp.exp(0.3 * vertical_profile[:, 0])[:, :, None])
    water2 = water1 - 0.5 * condensate
    cond_mean = jnp.mean(condensate, 2)
    crm_tend = jnp.stack(
        [
            2.0 * cond_mean,
            (jnp.mean(water2, 2) - jnp.mean(water, 2)) / 0.25,
            (jnp.mean(wind_x2, 2) - jnp.mean(wind_x, 2)) / 0.25,
            0.5 * cond_mean,
        ],
        1,
    )
    tendency = jnp.einsum("nfk,lk->nfl", crm_tend, down_map, precision=HIGH)
    tendency = tendency.reshape(column_count, 4 * levels).astype(jnp.bfloat16)
    fresh = (
        jnp.stack([wind_x2, wind_z2, water2], 1)
        .reshape(column_count, 3 * height * crm_width)
        .astype(jnp.bfloat16)
    )
    precip = 2.0 * jnp.mean(density[None, :] * cond_mean, 1)
    return (tendency, fresh, precip)


def edge_means(by_element):
    return 0.5 * jnp.stack(
        [
            by_element[:, 0] + by_element[:, 1],
            by_element[:, 1] + by_element[:, 3],
            by_element[:, 2] + by_element[:, 3],
            by_element[:, 0] + by_element[:, 2],
        ],
        1,
    )


def column_compactor(valid_flags, slot_capacity):
    length = valid_flags.shape[0]
    earlier = (jnp.arange(length)[:, None] < jnp.arange(length)[None, :]).astype(jnp.float32)
    position = jnp.dot(valid_flags, earlier, precision=HIGH).astype(jnp.int32)
    return (jnp.arange(slot_capacity, dtype=jnp.int32)[:, None] == position[None, :]) & (
        valid_flags[None, :] > 0.5
    )


def body(column_state, crm_fields, span_map, active, density, nbr_elem, nbr_side):
    levels = column_state.shape[1] // 4
    height = density.shape[0]
    crm_width = crm_fields.shape[1] // (3 * height)
    tables = make_tables(density, levels, height, crm_width)
    columns = column_state.shape[0]
    span_count = lax.axis_size("span")
    slot_capacity = columns * 3 // 8
    pair_depth = max(2, slot_capacity // span_count + 1)
    count_of_slots = span_count * pair_depth
    running = active > 0
    dest_hot = (
        (span_map[:, None] == jnp.arange(span_count, dtype=jnp.int32)[None, :]) & running[:, None]
    ).astype(jnp.float32)
    earlier = (jnp.arange(columns)[None, :] < jnp.arange(columns)[:, None]).astype(jnp.float32)
    before = jnp.dot(earlier, dest_hot, precision=HIGH)
    ranking = jnp.sum(before * dest_hot, 1).astype(jnp.int32)
    slot_index = span_map * pair_depth + ranking
    packing = (
        jnp.arange(count_of_slots, dtype=jnp.int32)[:, None] == slot_index[None, :]
    ) & running[None, :]
    pack_low = packing.astype(jnp.bfloat16)
    sent_valid = jnp.sum(packing.astype(jnp.float32), 1).reshape(span_count, pair_depth)
    sent_state = jnp.dot(pack_low, column_state, preferred_element_type=jnp.float32).astype(
        jnp.bfloat16
    )
    sent_fields = jnp.dot(pack_low, crm_fields, preferred_element_type=jnp.float32).astype(
        jnp.bfloat16
    )
    got_state, got_fields, received_valid = (
        lax.all_to_all(
            sent_state.reshape(span_count, pair_depth, -1),
            "span",
            split_axis=0,
            concat_axis=0,
            tiled=True,
        ),
        lax.all_to_all(
            sent_fields.reshape(span_count, pair_depth, -1),
            "span",
            split_axis=0,
            concat_axis=0,
            tiled=True,
        ),
        lax.all_to_all(
            sent_valid.astype(jnp.bfloat16), "span", split_axis=0, concat_axis=0, tiled=True
        ),
    )
    taken_columns = column_compactor(
        received_valid.reshape(count_of_slots).astype(jnp.float32), slot_capacity
    )
    take_low = taken_columns.astype(jnp.bfloat16)
    work_state = jnp.dot(
        take_low, got_state.reshape(count_of_slots, -1), preferred_element_type=jnp.float32
    ).astype(jnp.bfloat16)
    work_fields = jnp.dot(
        take_low, got_fields.reshape(count_of_slots, -1), preferred_element_type=jnp.float32
    ).astype(jnp.bfloat16)
    work_tend, work_fresh, work_precip = crm_step(
        work_state, work_fields, tables, levels, height, crm_width
    )
    span_precip = work_precip * jnp.sum(taken_columns.astype(jnp.float32), 1)
    back_tend = jnp.dot(take_low.T, work_tend, preferred_element_type=jnp.float32).astype(
        jnp.bfloat16
    )
    back_fresh = jnp.dot(take_low.T, work_fresh, preferred_element_type=jnp.float32).astype(
        jnp.bfloat16
    )
    ret_tend, ret_fresh = (
        lax.all_to_all(
            back_tend.reshape(span_count, pair_depth, -1),
            "span",
            split_axis=0,
            concat_axis=0,
            tiled=True,
        ),
        lax.all_to_all(
            back_fresh.reshape(span_count, pair_depth, -1),
            "span",
            split_axis=0,
            concat_axis=0,
            tiled=True,
        ),
    )
    tendency = jnp.dot(
        pack_low.T, ret_tend.reshape(count_of_slots, -1), preferred_element_type=jnp.float32
    ).astype(jnp.bfloat16)
    returned = jnp.dot(
        pack_low.T, ret_fresh.reshape(count_of_slots, -1), preferred_element_type=jnp.float32
    ).astype(jnp.bfloat16)
    fresh = jnp.where(running[:, None], returned, crm_fields)
    element_count = columns // 4
    by_element = tendency.astype(jnp.float32).reshape(element_count, 4, 4 * levels)
    edge_value = edge_means(by_element)
    halo_width = max(1, element_count // 2)
    widened = padded_2(
        edge_value.astype(jnp.bfloat16), ((("region", "span"), 0),), halo_width
    ).astype(edge_value.dtype)
    all_elems = element_count * lax.axis_size(("region", "span"))
    first_elem = lax.axis_index(("region", "span")) * element_count
    local_index = (nbr_elem - first_elem + halo_width + all_elems) % all_elems
    table_row = (local_index * 4 + nbr_side).reshape(-1)
    edge_table = widened.reshape(-1, 4 * levels)
    picking = (
        table_row[:, None] == jnp.arange(edge_table.shape[0], dtype=jnp.int32)[None, :]
    ).astype(jnp.float32)
    neighbour = jnp.dot(picking, edge_table, precision=HIGH).reshape(element_count, 4, 4 * levels)
    edge_sums = edge_value + neighbour
    return (tendency, fresh, span_precip, edge_sums)


def solution(mesh):
    in_specs = (
        P(("region", "span"), None),
        P(("region", "span"), None),
        P(("region", "span")),
        P(("region", "span")),
        P(),
        P(("region", "span"), None),
        P(("region", "span"), None),
    )
    out_specs = (
        P(("region", "span"), None),
        P(("region", "span"), None),
        P(("region", "span")),
        P(("region", "span"), None, None),
    )
    return jax.shard_map(body, mesh=mesh, in_specs=in_specs, out_specs=out_specs, check_vma=False)
```

profile of v0, /device:TPU:6, one launch (start us, length us, event | category | flops | bytes accessed | tf_op | source)
XLA Modules:
  0.0 534.9 jit_solution(9698388515154535200)
XLA Ops:
  3.7 28.7 %all-to-all-start = ((bf16[32,1,2]{2,1,0:T(2,128)(2,1)}), bf16[32,1,2]{2,1,0:T(2,128)(2,1)S(1)}, u32[]{:S(2)}, u32[]{:S(2)}) async-start(bf16[32,1,2]{2,1,0:T(2,128)(2,1)} %convert_element_type.144), calls=%async_computation | async-start | bytes 32768 | tf_op jit(solution)/shard_map/all_to_all | solution.py:198
  33.8 1.4 convolution_convert_fusion.1
  37.6 17.2 %all-to-all-done = bf16[32,1,2]{2,1,0:T(2,128)(2,1)S(1)} async-done(((bf16[32,1,2]{2,1,0:T(2,128)(2,1)}), bf16[32,1,2]{2,1,0:T(2,128)(2,1)S(1)}, u32[]{:S(2)}, u32[]{:S(2)}) %all-to-all-start) | async-done | bytes 160 | tf_op jit(solution)/shard_map/all_to_all | solution.py:198
  54.8 4.6 all-to-all-start.2
  60.0 23.3 %all-to-all-done.2 = bf16[32,2,288]{2,1,0:T(2,128)(2,1)S(1)} async-done(((bf16[32,2,288]{2,1,0:T(2,128)(2,1)}), bf16[32,2,288]{2,1,0:T(2,128)(2,1)S(1)}, u32[]{:S(2)}, u32[]{:S(2)}) %all-to-all-start.2) | async-done | bytes 36896 | tf_op jit(solution)/shard_map/all_to_all | solution.py:184
  83.3 4.1 all-to-all-start.1
  93.1 1.8 broadcast_multiply_fusion.2
  95.6 32.0 %divide_bitcast_fusion = (f32[32]{0:T(128)}, f32[1,32]{1,0:T(1,128)}, f32[32,1]{0,1:T(1,128)S(1)}) fusion(f32[]{:T(128)} %bitcast.28, f32[]{:T(128)} %bitcast.32, f32[]{:T(128)} %bitcast.35, f32[]{:T(128)} %bitcast.38, f32[]{:T(128)} %bitcast.41, f32[]{:T(128)} %bitcast.44, f32[]{:T(128)} %bitcast.47, f32[]{:T(128)} %bitcast.50, f32[]{:T(128)} %bitcast.53, ...), kind=kLoop, calls=%fused_computation.787 | loop fusion | flops 2432 | bytes 3916 | tf_op jit(solution)/shard_map/vmap()/while/body/eval_jaxpr/mul | solution.py:106
  127.6 51.9 %fusion.433 = (f32[32]{0:T(128)}, f32[32,1]{0,1:T(1,128)S(1)}, f32[32,1]{0,1:T(1,128)S(1)}, f32[32,1]{0,1:T(1,128)S(1)}, f32[32,1]{0,1:T(1,128)S(1)}, /*index=5*...) fusion(f32[]{:T(128)} %bitcast.270, ...), kind=kLoop, calls=%fused_computation.913 | loop fusion | flops 3968 | bytes 11208 | tf_op jit(solution)/shard_map/vmap()/eval_jaxpr/sub | solution.py:106
  179.8 3.6 fusion.403
  183.4 5.1 fusion.376
  188.5 4.4 fusion.398
  192.9 4.3 fusion.399
  197.2 4.3 fusion.400
  201.5 4.3 fusion.401
  205.8 4.4 fusion.402
  210.3 71.8 %fusion.318 = (f32[32]{0:T(128)S(1)}, f32[32]{0:T(128)S(1)}, f32[32]{0:T(128)}, f32[32]{0:T(128)}, f32[32]{0:T(128)}, /*index=5*/f32[32]{0:T(128)S(1)}, f32[32]{...) fusion(f32[57,32]{1,0:T(8,128)S(1)} %slice_bitcast_fusion.1, ...), kind=kLoop, calls=%fused_computation.620 | loop fusion | flops 5472 | bytes 11592 | tf_op jit(solution)/shard_map/vmap()/eval_jaxpr/sub | solution.py:106
  285.2 1.6 slice_reduce_fusion
  286.8 1.5 copy.5962
  294.1 37.3 %fusion.296 = (f32[32,1,24]{0,2,1:T(8,128)S(1)}, f32[1,32,24]{1,2,0:T(8,128)S(1)}, f32[1,32,24]{1,2,0:T(8,128)S(1)}, f32[1,32,24]{1,2,0:T(8,128)S(1)}, f32[1,32,...) fusion(f32[57,32,24]{1,2,0:T(8,128)S(1)} %slice_bitcast_fusion,, ...), kind=kLoop, calls=%fused_computation.491 | loop fusion | flops 278016 | bytes 869888 | tf_op jit(solution)/shard_map/vmap()/eval_jaxpr/sub | solution.py:106
  331.8 28.8 %constant_dynamic-update-slice_fusion.56 = (f32[57,32,24]{1,2,0:T(8,128)S(1)}, f32[1,32,24]{1,2,0:T(8,128)S(1)}, f32[1,32,24]{1,2,0:T(8,128)S(1)}, f32[1,32,24]{...) fusion(f32[1,32,24]{1,2,0:T(8,128)S(1)} %get-tuple-element.207,, ...), kind=kLoop, calls=%fused_computation.127 | loop fusion | flops 187391 | bytes 556720
  362.2 36.8 %constant_dynamic-update-slice_fusion.14 = (f32[57,32,24]{1,2,0:T(8,128)S(1)}, f32[32,24]{0,1:T(8,128)S(1)}, f32[32,24]{0,1:T(8,128)S(1)}, f32[32,24]{0,1:T(8,12...) fusion(f32[57,32,24]{1,2,0:T(8,128)S(1)} %constant_dynamic-upda, ...), kind=kLoop, calls=%fused_computation.85 | loop fusion | flops 153600 | bytes 914148
  400.5 2.3 convolution_bitcast_fusion
  404.9 21.8 %all-to-all-start.3 = ((bf16[32,2,288]{2,1,0:T(2,128)(2,1)}), bf16[32,2,288]{2,1,0:T(2,128)(2,1)S(1)}, u32[]{:S(2)}, u32[]{:S(2)}) async-start(bf16[32,2,288]{2,1,0:T(2,128)(2,1)} %reshape.49536), calls=%async_computation.3 | async-start | bytes 98304 | tf_op jit(solution)/shard_map/all_to_all | solution.py:223
  429.3 1.1 reshape.49538
  430.5 20.1 %all-to-all-done.3 = bf16[32,2,288]{2,1,0:T(2,128)(2,1)S(1)} async-done(((bf16[32,2,288]{2,1,0:T(2,128)(2,1)}), bf16[32,2,288]{2,1,0:T(2,128)(2,1)S(1)}, u32[]{:S(2)}, u32[]{:S(2)}) %all-to-all-start.3) | async-done | bytes 36896 | tf_op jit(solution)/shard_map/all_to_all | solution.py:223
  450.5 3.9 all-to-all-start.4
  455.1 3.1 collective-permute-start.1
  458.1 2.9 collective-permute-start
  461.6 47.8 %collective-permute-done.1 = bf16[8,4,288]{2,0,1:T(8,128)(2,1)S(1)} collective-permute-done((bf16[8,4,288]{2,0,1:T(8,128)(2,1)S(1)}, bf16[8,4,288]{2,0,1:T(8,128)(2,1)S(1)}, u32[]{:S(2)}, u32[]{:S(2)}) %collective-permute-start.1) | collective-permute-done | bytes 18464 | tf_op jit(solution)/shard_map/ppermute | solution.py:18
  510.4 22.7 %all-to-all-done.4 = bf16[32,2,5568]{2,1,0:T(2,128)(2,1)S(1)} async-done(((bf16[32,2,5568]{2,1,0:T(2,128)(2,1)}), bf16[32,2,5568]{2,1,0:T(2,128)(2,1)S(1)}, u32[]{:S(2)}, u32[]{:S(2)}) %all-to-all-start.4) | async-done | bytes 712736 | tf_op jit(solution)/shard_map/all_to_all | solution.py:230
  533.6 1.3 fusion
  (412 shorter events, 31.3 us)
Async XLA Ops:
  3.7 51.1 %all-to-all-start = ((bf16[32,1,2]{2,1,0:T(2,128)(2,1)}), bf16[32,1,2]{2,1,0:T(2,128)(2,1)S(1)}, u32[]{:S(2)}, u32[]{:S(2)}) async-start(bf16[32,1,2]{2,1,0:T(2,128)(2,1)} %convert_element_type.144), calls=%async_computation | async-start | bytes 32768 | tf_op jit(solution)/shard_map/all_to_all | solution.py:198
  54.8 28.5 %all-to-all-start.2 = ((bf16[32,2,288]{2,1,0:T(2,128)(2,1)}), bf16[32,2,288]{2,1,0:T(2,128)(2,1)S(1)}, u32[]{:S(2)}, u32[]{:S(2)}) async-start(bf16[32,2,288]{2,1,0:T(2,128)(2,1)} %reshape.49533), calls=%async_computation.2 | async-start | bytes 98304 | tf_op jit(solution)/shard_map/all_to_all | solution.py:184
  83.3 200.1 %all-to-all-start.1 = ((bf16[32,2,5568]{2,1,0:T(2,128)(2,1)}), bf16[32,2,5568]{2,1,0:T(2,128)(2,1)S(1)}, u32[]{:S(2)}, u32[]{:S(2)}) async-start(bf16[32,2,5568]{2,1,0:T(2,128)(2,1)} %reshape.49529), calls=%async_computation.1 | async-start | bytes 1441792 | tf_op jit(solution)/shard_map/all_to_all | solution.py:191
  179.6 103.0 %copy-start.27 = (f32[32,1]{0,1:T(1,128)}, f32[32,1]{0,1:T(1,128)S(1)}, u32[]{:S(2)}) copy-start(f32[32,1]{0,1:T(1,128)S(1)} %get-tuple-element.276) | copy-start | bytes 388
  179.6 102.9 %copy-start.29 = (f32[32,1]{0,1:T(1,128)}, f32[32,1]{0,1:T(1,128)S(1)}, u32[]{:S(2)}) copy-start(f32[32,1]{0,1:T(1,128)S(1)} %get-tuple-element.278) | copy-start | bytes 388
  179.6 102.9 %copy-start.31 = (f32[32,1]{0,1:T(1,128)}, f32[32,1]{0,1:T(1,128)S(1)}, u32[]{:S(2)}) copy-start(f32[32,1]{0,1:T(1,128)S(1)} %get-tuple-element.280) | copy-start | bytes 388
  179.6 103.5 %copy-start.43 = (f32[32,1]{0,1:T(1,128)}, f32[32,1]{0,1:T(1,128)S(1)}, u32[]{:S(2)}) copy-start(f32[32,1]{0,1:T(1,128)S(1)} %get-tuple-element.288) | copy-start | bytes 388
  179.6 103.5 %copy-start.46 = (f32[32,1]{0,1:T(1,128)}, f32[32,1]{0,1:T(1,128)S(1)}, u32[]{:S(2)}) copy-start(f32[32,1]{0,1:T(1,128)S(1)} %get-tuple-element.290) | copy-start | bytes 388
  179.6 103.5 %copy-start.49 = (f32[32,1]{0,1:T(1,128)}, f32[32,1]{0,1:T(1,128)S(1)}, u32[]{:S(2)}) copy-start(f32[32,1]{0,1:T(1,128)S(1)} %get-tuple-element.292) | copy-start | bytes 388
  179.7 103.5 %copy-start.52 = (f32[32,1]{0,1:T(1,128)}, f32[32,1]{0,1:T(1,128)S(1)}, u32[]{:S(2)}) copy-start(f32[32,1]{0,1:T(1,128)S(1)} %get-tuple-element.294) | copy-start | bytes 388
  179.7 103.5 %copy-start.97 = (f32[32,1]{0,1:T(1,128)}, f32[32,1]{0,1:T(1,128)S(1)}, u32[]{:S(2)}) copy-start(f32[32,1]{0,1:T(1,128)S(1)} %get-tuple-element.257) | copy-start | bytes 388
  179.7 103.5 %copy-start.98 = (f32[32,1]{0,1:T(1,128)}, f32[32,1]{0,1:T(1,128)S(1)}, u32[]{:S(2)}) copy-start(f32[32,1]{0,1:T(1,128)S(1)} %get-tuple-element.259) | copy-start | bytes 388
  179.7 103.5 %copy-start.99 = (f32[32,1]{0,1:T(1,128)}, f32[32,1]{0,1:T(1,128)S(1)}, u32[]{:S(2)}) copy-start(f32[32,1]{0,1:T(1,128)S(1)} %get-tuple-element.261) | copy-start | bytes 388
  179.7 103.5 %copy-start.100 = (f32[32,1]{0,1:T(1,128)}, f32[32,1]{0,1:T(1,128)S(1)}, u32[]{:S(2)}) copy-start(f32[32,1]{0,1:T(1,128)S(1)} %get-tuple-element.263) | copy-start | bytes 388
  179.7 103.5 %copy-start.101 = (f32[32,1]{0,1:T(1,128)}, f32[32,1]{0,1:T(1,128)S(1)}, u32[]{:S(2)}) copy-start(f32[32,1]{0,1:T(1,128)S(1)} %get-tuple-element.265) | copy-start | bytes 388
  179.7 103.5 %copy-start.102 = (f32[32,1]{0,1:T(1,128)}, f32[32,1]{0,1:T(1,128)S(1)}, u32[]{:S(2)}) copy-start(f32[32,1]{0,1:T(1,128)S(1)} %get-tuple-element.267) | copy-start | bytes 388
  179.7 103.5 %copy-start.103 = (f32[32,1]{0,1:T(1,128)}, f32[32,1]{0,1:T(1,128)S(1)}, u32[]{:S(2)}) copy-start(f32[32,1]{0,1:T(1,128)S(1)} %get-tuple-element.269) | copy-start | bytes 388
  179.7 103.5 %copy-start.104 = (f32[32,1]{0,1:T(1,128)}, f32[32,1]{0,1:T(1,128)S(1)}, u32[]{:S(2)}) copy-start(f32[32,1]{0,1:T(1,128)S(1)} %get-tuple-element.271) | copy-start | bytes 388
  179.7 103.5 %copy-start.105 = (f32[32,1]{0,1:T(1,128)}, f32[32,1]{0,1:T(1,128)S(1)}, u32[]{:S(2)}) copy-start(f32[32,1]{0,1:T(1,128)S(1)} %get-tuple-element.273) | copy-start | bytes 388
  179.8 103.5 %copy-start.106 = (f32[32,1]{0,1:T(1,128)}, f32[32,1]{0,1:T(1,128)S(1)}, u32[]{:S(2)}) copy-start(f32[32,1]{0,1:T(1,128)S(1)} %get-tuple-element.275) | copy-start | bytes 388
  179.8 103.5 %copy-start.107 = (f32[32,1]{0,1:T(1,128)}, f32[32,1]{0,1:T(1,128)S(1)}, u32[]{:S(2)}) copy-start(f32[32,1]{0,1:T(1,128)S(1)} %get-tuple-element.277) | copy-start | bytes 388
  179.8 103.5 %copy-start.108 = (f32[32,1]{0,1:T(1,128)}, f32[32,1]{0,1:T(1,128)S(1)}, u32[]{:S(2)}) copy-start(f32[32,1]{0,1:T(1,128)S(1)} %get-tuple-element.279) | copy-start | bytes 388
  179.8 103.5 %copy-start.109 = (f32[32,1]{0,1:T(1,128)}, f32[32,1]{0,1:T(1,128)S(1)}, u32[]{:S(2)}) copy-start(f32[32,1]{0,1:T(1,128)S(1)} %get-tuple-element.281) | copy-start | bytes 388
  179.8 103.5 %copy-start.110 = (f32[32,1]{0,1:T(1,128)}, f32[32,1]{0,1:T(1,128)S(1)}, u32[]{:S(2)}) copy-start(f32[32,1]{0,1:T(1,128)S(1)} %get-tuple-element.283) | copy-start | bytes 388
  179.8 103.5 %copy-start.111 = (f32[32,1]{0,1:T(1,128)}, f32[32,1]{0,1:T(1,128)S(1)}, u32[]{:S(2)}) copy-start(f32[32,1]{0,1:T(1,128)S(1)} %get-tuple-element.285) | copy-start | bytes 388
  179.8 103.5 %copy-start.112 = (f32[32,1]{0,1:T(1,128)}, f32[32,1]{0,1:T(1,128)S(1)}, u32[]{:S(2)}) copy-start(f32[32,1]{0,1:T(1,128)S(1)} %get-tuple-element.287) | copy-start | bytes 388
  179.8 103.5 %copy-start.113 = (f32[32,1]{0,1:T(1,128)}, f32[32,1]{0,1:T(1,128)S(1)}, u32[]{:S(2)}) copy-start(f32[32,1]{0,1:T(1,128)S(1)} %get-tuple-element.289) | copy-start | bytes 388
  179.8 103.5 %copy-start.114 = (f32[32,1]{0,1:T(1,128)}, f32[32,1]{0,1:T(1,128)S(1)}, u32[]{:S(2)}) copy-start(f32[32,1]{0,1:T(1,128)S(1)} %get-tuple-element.291) | copy-start | bytes 388
  404.9 45.6 %all-to-all-start.3 = ((bf16[32,2,288]{2,1,0:T(2,128)(2,1)}), bf16[32,2,288]{2,1,0:T(2,128)(2,1)S(1)}, u32[]{:S(2)}, u32[]{:S(2)}) async-start(bf16[32,2,288]{2,1,0:T(2,128)(2,1)} %reshape.49536), calls=%async_computation.3 | async-start | bytes 98304 | tf_op jit(solution)/shard_map/all_to_all | solution.py:223
  450.5 82.6 %all-to-all-start.4 = ((bf16[32,2,5568]{2,1,0:T(2,128)(2,1)}), bf16[32,2,5568]{2,1,0:T(2,128)(2,1)S(1)}, u32[]{:S(2)}, u32[]{:S(2)}) async-start(bf16[32,2,5568]{2,1,0:T(2,128)(2,1)} %reshape.49538), calls=%async_computation.4 | async-start | bytes 1441792 | tf_op jit(solution)/shard_map/all_to_all | solution.py:230
  455.1 54.4 %collective-permute-start.1 = (bf16[8,4,288]{2,0,1:T(8,128)(2,1)S(1)}, bf16[8,4,288]{2,0,1:T(8,128)(2,1)S(1)}, u32[]{:S(2)}, u32[]{:S(2)}) collective-permute-start(bf16[8,4,288]{2,0,1:T(8,128)(2,1)S(1)} %get-tuple-element.362), channel_id=1, source_target_pairs={{1,0},{2,1},{3,2},{4,3},{5,4},{6,5},{7,6},{8,7},{9,8},{10,9},{11,1... | collective-permute-start | bytes 55304 | tf_op jit(solution)/shard_map/ppermute | solution.py:18
  458.1 51.3 %collective-permute-start = (bf16[8,4,288]{2,0,1:T(8,128)(2,1)S(1)}, bf16[8,4,288]{2,0,1:T(8,128)(2,1)S(1)}, u32[]{:S(2)}, u32[]{:S(2)}) collective-permute-start(bf16[8,4,288]{2,0,1:T(8,128)(2,1)S(1)} %get-tuple-element.361), channel_id=1, source_target_pairs={{0,1},{1,2},{2,3},{3,4},{4,5},{5,6},{6,7},{7,8},{8,9},{9,10},{10,1... | collective-permute-start | bytes 55304 | tf_op jit(solution)/shard_map/ppermute | solution.py:16
  (107 other events, 2445.3 us)
where the time goes:
time: 540 us; the launch traced here: 535 us
  other arithmetic  302 us (56%)
  waiting for transfers between devices  131 us (24%)
  starting transfers between devices  69.1 us (13%)
  local copies, waits for them, and re-layouts  20.5 us (4%)
  matrix products  8.7 us (2%)
    sub x10, other arithmetic, crm_step(): lax.linalg.tridiagonal_solve(lower_diag, main_diag, upper_diag, spectrum)  191 us
    unnamed x29, other arithmetic  67 us
    ppermute x1, waiting for transfers between devices, padded_2(): lax.ppermute(head, axis, [((i + 1) % count, i) for i in range(count)])  47.8 us
    mul x1, other arithmetic, crm_step(): lax.linalg.tridiagonal_solve(lower_diag, main_diag, upper_diag, spectrum)  32 us
    all_to_all x1, starting transfers between devices, body(): lax.all_to_all(sent_valid.astype(jnp.bfloat16), 'span', split_axis=0, con...  28.7 us
    all_to_all x1, waiting for transfers between devices, body(): lax.all_to_all(sent_state.reshape(span_count, pair_depth, -1), 'span', sp...  23.3 us
    all_to_all x1, waiting for transfers between devices, body(): lax.all_to_all(back_fresh.reshape(span_count, pair_depth, -1), 'span', sp...  22.7 us
    all_to_all x1, starting transfers between devices, body(): lax.all_to_all(back_tend.reshape(span_count, pair_depth, -1), 'span', spl...  21.8 us
  transfers between devices with their start and end apart: 7, of which 5 were waited for; matrix products, arithmetic and copies ran while one was open for 39% of the time, Pallas kernels for 0%

commit v1 on v0

v1 whole, which is shorter than its diff:
```python
import functools

import jax
import jax.numpy as jnp
import ml_dtypes
import numpy as np
from jax import lax
from jax.experimental import pallas as pl
from jax.experimental.pallas import tpu as pltpu
from jax.sharding import PartitionSpec as P

HIGH = lax.Precision.HIGHEST
LEV, NZ, NX, COLS = 72, 58, 32, 64
G, R, LANES = 4, 16, 128
ROWS = NZ * R
PAD = (NZ + 2) * R
F32, BF16 = jnp.float32, jnp.bfloat16


def split(a):
    high = a.astype(ml_dtypes.bfloat16)
    return high, (a - high.astype(np.float64)).astype(ml_dtypes.bfloat16)


def level_map(count_to, count_from):
    index = np.arange(count_to)
    numerator = (2 * index + 1) * count_from - count_to
    lower = np.clip(numerator // (2 * count_to), 0, count_from - 2)
    fraction = np.clip((numerator - lower * 2 * count_to) / (2 * count_to), 0.0, 1.0)
    target = np.arange(count_from)[None, :]
    return (1 - fraction)[:, None] * (target == lower[:, None]) + fraction[:, None] * (
        target == lower[:, None] + 1
    )


@functools.cache
def tables():
    eye = np.eye(G)
    step = 0.5 * (np.roll(np.eye(NX), 1, 0) - np.roll(np.eye(NX), -1, 0))
    dxm = np.concatenate(
        [np.kron(eye, 0.25 * step), np.kron(eye, np.full((NX, NX), 0.25 / NX))], 1
    ).astype(ml_dtypes.bfloat16)
    mode = np.arange(NX)
    wave = np.where(mode <= NX // 2, mode, mode - NX // 2)
    phase = 2 * np.pi * (wave[:, None] * np.arange(NX)[None, :] % NX) / NX
    norm = np.where((mode == 0) | (mode == NX // 2), np.sqrt(1 / NX), np.sqrt(2 / NX))
    four = norm[:, None] * np.where((mode <= NX // 2)[:, None], np.cos(phase), np.sin(phase))
    eigen = np.tile(2 - 2 * np.cos(2 * np.pi * wave / NX), G)[None, :]
    eigen = np.broadcast_to(eigen, (R, LANES)).astype(np.float32)

    def doubled(a):
        return np.concatenate(split(a), 1)

    to_mode = -four.T
    forward = np.concatenate(
        [doubled(np.kron(eye, a)) for a in (step @ to_mode, step @ to_mode, to_mode, to_mode)], 0
    )
    back = np.concatenate([np.kron(eye, 0.5 * four), np.kron(eye, four @ step)], 1)
    back = np.concatenate([doubled(back)] * 2, 0)
    up = level_map(NZ, LEV)
    zero = np.zeros_like(up)
    blocks = [
        [0.3 * up, zero, zero, zero],
        [zero, 0.25 * up, zero, 0.25 * up],
        [zero, zero, 0.25 * up, zero],
    ]
    rise = np.zeros((192, 4 * LEV))
    for i, row in enumerate(blocks):
        rise[64 * i : 64 * i + NZ] = np.concatenate(row, 1)
    rise = np.stack(split(rise))
    column, lane = np.arange(LANES) % COLS, np.arange(LANES)
    spread = (column[:, None] // R == lane[None, :] // NX).astype(ml_dtypes.bfloat16)
    gather = (lane[:, None] // NX == column[None, :] // R) / NX
    gather = np.concatenate([gather, gather], 0).astype(ml_dtypes.bfloat16)
    tally = np.zeros((64, ROWS))
    for z in range(NZ):
        tally[z, R * z : R * z + R] = 1
    tally = tally.astype(ml_dtypes.bfloat16)
    down = level_map(LEV, NZ)
    fall = np.zeros((4 * LEV, 192))
    for f, (source, gain) in enumerate(((0, 2.0), (1, 4.0), (2, 4.0), (0, 0.5))):
        fall[LEV * f : LEV * f + LEV, 64 * source : 64 * source + NZ] = gain * down
    fall = fall.astype(np.float32)
    return dxm, forward, back, eigen, rise, spread, gather, tally, fall


def dot(a, b, dims=((1,), (0,)), precision=None):
    return lax.dot_general(a, b, (dims, ((), ())), precision=precision, preferred_element_type=F32)


def halves(a):
    high = a.astype(BF16)
    return high, (a - high.astype(F32)).astype(BF16)


def regroup(parts):
    lane = lax.broadcasted_iota(jnp.int32, (R, LANES), 1)
    low, even = lane < 64, (lane & 32) == 0
    a, b, c, d = parts
    a, c = jnp.where(low, a, pltpu.roll(c, 64, 1)), jnp.where(low, pltpu.roll(a, 64, 1), c)
    b, d = jnp.where(low, b, pltpu.roll(d, 64, 1)), jnp.where(low, pltpu.roll(b, 64, 1), d)
    a, b = jnp.where(even, a, pltpu.roll(b, 32, 1)), jnp.where(even, pltpu.roll(a, 96, 1), b)
    c, d = jnp.where(even, c, pltpu.roll(d, 32, 1)), jnp.where(even, pltpu.roll(c, 96, 1), d)
    return a, b, c, d


def at(z):
    return pl.ds(pl.multiple_of(z * R, R), R)


def crm_kernel(
    state_ref, fields_ref, active_ref, density_ref, density_row_ref,
    dxm_ref, forward_ref, back_ref, eigen_ref, rise_ref, spread_ref, gather_ref, tally_ref, fall_ref,
    tend_ref, fresh_ref, precip_ref,
    raw, dxm, prof, prof_wide, prof_rows, inv, coupling, u1, w1, left, sol, sol_low, pres, means, fresh,
):
    lane = lax.broadcasted_iota(jnp.int32, (R, LANES), 1)
    row = lax.broadcasted_iota(jnp.int32, (R, LANES), 0)
    own = (lane & (R - 1)) == row

    zero16 = jnp.zeros((R, LANES), BF16)
    for f in range(3):
        raw[f, :R] = zero16
        raw[f, R * (NZ + 1) :] = zero16
    for j in range(44):
        if j < 43:
            parts = [fields_ref[R * g : R * g + R, LANES * j : LANES * j + LANES] for g in range(G)]
        else:
            parts = [
                jnp.concatenate(
                    [fields_ref[R * g : R * g + R, LANES * j :], jnp.zeros((R, 64), BF16)], 1
                )
                for g in range(G)
            ]
        for part, level in zip(regroup(parts), range(4 * j, min(4 * j + 4, 3 * NZ))):
            f, z = divmod(level, NZ)
            raw[f, R * (z + 1) : R * (z + 2)] = part
    for f in range(3):
        dxm[f] = dot(raw[f, R : R + ROWS], dxm_ref[...])

    state = state_ref[...]
    profile = dot(rise_ref[0], state, ((1,), (1,))) + dot(rise_ref[1], state, ((1,), (1,)))
    prof[:64] = jnp.exp(profile[:64])
    prof[64:] = profile[64:]
    flags = active_ref[...].reshape(1, COLS).astype(F32)
    prof[63:64] = flags
    p_high, p_low = halves(prof[...])
    prof_wide[...] = jnp.concatenate([p_high, p_low], 1).astype(F32)

    @pl.loop(0, 192, unroll=4)
    def _(i):
        line = jnp.broadcast_to(prof_wide[pl.ds(i, 1)], (R, LANES))
        prof_rows[at(i)] = jnp.where(own, line, 0.0).astype(BF16)

    for f in range(3):
        block = dot(prof_rows[64 * R * f : 64 * R * (f + 1)], spread_ref[...])
        means[f] = block
    mask = means[0, 63 * R :] > 0.5

    eigen = eigen_ref[...]

    def factor(z, last):
        rho = density_ref[z]
        above = jnp.where(z < NZ - 1, density_ref[jnp.minimum(z + 1, NZ - 1)], rho)
        below = jnp.where(z > 0, density_ref[jnp.maximum(z - 1, 0)], rho)
        f_up, f_down = 0.5 * (rho + above), 0.5 * (rho + below)
        before = jnp.where(z > 0, f_down, 0.0)
        i = 1.0 / ((eigen * rho + (f_up + f_down)) - before * last)
        e = jnp.where(z < NZ - 1, f_up, 0.0) * i
        inv[at(z)] = i
        coupling[at(z + 1)] = e
        return e

    coupling[:R] = jnp.zeros((R, LANES), F32)
    lax.fori_loop(0, NZ, factor, coupling[:R])

    def load(f, z):
        return raw[f, at(z)].astype(F32)

    zero = coupling[:R]

    def advect(z, carry):
        (u_m, u), (w_m, w), (q_m, q), (rw_mm, rw_m) = carry
        here = at(z)
        u_p, w_p, q_p = load(0, z + 2), load(1, z + 2), load(2, z + 2)
        rho = density_ref[z]
        half = 0.125 * w
        mean_u, mean_q = dxm[0, here, LANES:], dxm[2, here, LANES:]
        new_u = u - u * dxm[0, here, :LANES] - half * (u_p - u_m) + (means[2, here] - mean_u)
        new_w = w - u * dxm[1, here, :LANES] - half * (w_p - w_m) + (0.125 * q - 0.5 * mean_q)
        new_q = q - u * dxm[2, here, :LANES] - half * (q_p - q_m) + (means[1, here] - mean_q)
        x = new_q - means[0, here]
        cond = jnp.maximum(x, 0.0) + jnp.log(1.0 + jnp.exp(-jnp.abs(x)))
        q2 = new_q - 0.5 * cond
        u1[here] = new_u
        w1[at(z + 1)] = new_w
        fresh[at(2 * NZ + z)] = jnp.where(mask, q2, q).astype(BF16)
        high, low = halves(cond)
        sol_low[0, here, :LANES], sol_low[0, here, LANES:] = high, low
        high, low = halves(q2 - q)
        sol_low[1, here, :LANES], sol_low[1, here, LANES:] = high, low
        high, low = halves(rho * new_u)
        left[at(z + 1), :LANES], left[at(z + 1), LANES : 2 * LANES] = high, low
        rw = rho * new_w
        high, low = halves(0.5 * (rw - rw_mm))
        left[at(z), 2 * LANES : 3 * LANES], left[at(z), 3 * LANES :] = high, low
        return (u, u_p), (w, w_p), (q, q_p), (rw_m, rw)

    first = tuple((zero, load(f, 1)) for f in range(3)) + ((zero, zero),)
    *_, (rw_m, _) = lax.fori_loop(0, NZ, advect, first)
    high, low = halves(-0.5 * rw_m)
    left[at(NZ), 2 * LANES : 3 * LANES], left[at(NZ), 3 * LANES :] = high, low

    right = dot(left[R:], forward_ref[...])
    sol[...] = right[:, :LANES] + right[:, LANES:]

    def sweep_up(z, last):
        last = sol[at(z)] + coupling[at(z)] * last
        sol[at(z)] = last
        return last

    lax.fori_loop(0, NZ, sweep_up, zero, unroll=2)

    def sweep_down(i, last):
        z = NZ - 1 - i
        last = inv[at(z)] * sol[at(z)] + coupling[at(z + 1)] * last
        high, low = halves(last)
        left[at(z), :LANES], left[at(z), LANES : 2 * LANES] = high, low
        return last

    lax.fori_loop(0, NZ, sweep_down, zero, unroll=2)
    both = dot(left[:ROWS, : 2 * LANES], back_ref[...])
    pres[:R] = zero
    pres[R * (NZ + 1) :] = zero
    pres[R : R + ROWS] = both[:, :LANES] + both[:, 2 * LANES : 3 * LANES]
    sol[...] = both[:, LANES : 2 * LANES] + both[:, 3 * LANES :]

    @pl.loop(0, NZ)
    def _(z):
        here = at(z)
        u, w = load(0, z + 1), load(1, z + 1)
        u2 = u1[here] - sol[here]
        w2 = w1[at(z + 1)] - (pres[at(z + 2)] - pres[here])
        fresh[here] = jnp.where(mask, u2, u).astype(BF16)
        fresh[at(NZ + z)] = jnp.where(mask, w2, w).astype(BF16)
        high, low = halves(u2 - u)
        sol_low[2, here, :LANES], sol_low[2, here, LANES:] = high, low

    lane_high = lane < COLS
    sums = []
    for f in range(3):
        means[f, :ROWS] = dot(sol_low[f], gather_ref[...])

        @pl.loop(0, NZ)
        def _(z):
            value = jnp.where(own, means[f, at(z)], 0.0)
            high = value.astype(BF16)
            low = (value - high.astype(F32)).astype(BF16)
            left[at(z), :LANES] = jnp.where(lane_high, high, low)

        total = dot(tally_ref[...], left[:ROWS, :LANES])
        sums.append(total[:, :COLS] + total[:, COLS:])
    tend = dot(fall_ref[...], jnp.concatenate(sums, 0), precision=HIGH)
    tend = jnp.where(flags > 0.5, tend, 0.0)
    tend_ref[...] = tend.T.astype(BF16)
    weights = density_row_ref[...] * (2.0 / NZ)
    precip_ref[...] = dot(weights, sums[0][:NZ], precision=HIGH)

    for j in range(44):
        parts = [
            fresh[R * level : R * level + R] if level < 3 * NZ else zero16
            for level in range(4 * j, 4 * j + 4)
        ]
        for g, part in enumerate(regroup(parts)):
            if j < 43:
                fresh_ref[R * g : R * g + R, LANES * j : LANES * j + LANES] = part
            else:
                fresh_ref[R * g : R * g + R, LANES * j :] = part[:, :64]


def crm_call(column_state, crm_fields, active, density):
    constants = [jnp.asarray(a) for a in tables()]
    vmem = pl.BlockSpec(memory_space=pltpu.VMEM)
    smem = pl.BlockSpec(memory_space=pltpu.SMEM)
    return pl.pallas_call(
        crm_kernel,
        out_shape=(
            jax.ShapeDtypeStruct((COLS, 4 * LEV), BF16),
            jax.ShapeDtypeStruct((COLS, 3 * NZ * NX), BF16),
            jax.ShapeDtypeStruct((1, COLS), F32),
        ),
        in_specs=[vmem, vmem, vmem, smem, vmem] + [vmem] * len(constants),
        out_specs=(vmem, vmem, vmem),
        scratch_shapes=[
            pltpu.VMEM((3, PAD, LANES), BF16),
            pltpu.VMEM((3, ROWS, 2 * LANES), F32),
            pltpu.VMEM((192, COLS), F32),
            pltpu.VMEM((192, LANES), F32),
            pltpu.VMEM((192 * R, LANES), BF16),
            pltpu.VMEM((ROWS, LANES), F32),
            pltpu.VMEM((PAD, LANES), F32),
            pltpu.VMEM((ROWS, LANES), F32),
            pltpu.VMEM((PAD, LANES), F32),
            pltpu.VMEM((ROWS + R, 4 * LANES), BF16),
            pltpu.VMEM((ROWS, LANES), F32),
            pltpu.VMEM((3, ROWS, 2 * LANES), BF16),
            pltpu.VMEM((PAD, LANES), F32),
            pltpu.VMEM((3, 64 * R, LANES), F32),
            pltpu.VMEM((3 * ROWS, LANES), BF16),
        ],
        compiler_params=pltpu.CompilerParams(vmem_limit_bytes=48 * 2**20),
    )(column_state, crm_fields, active, density, density.reshape(1, NZ), *constants)


def edge_part(tendency, nbr_elem, nbr_side):
    axes = ("region", "span")
    count = lax.axis_size(axes)
    up = [(i, (i + 1) % count) for i in range(count)]
    down = [((i + 1) % count, i) for i in range(count)]
    half = COLS // 2
    table = jnp.concatenate(
        [
            lax.ppermute(tendency[half:], axes, up),
            tendency,
            lax.ppermute(tendency[:half], axes, down),
        ],
        0,
    )
    elems = COLS // 4
    first = lax.axis_index(axes) * elems
    near = (nbr_elem - first + elems // 2 + elems * count) % (elems * count)
    sides = jnp.arange(4, dtype=jnp.int32)
    corner = jnp.array([[1, 1, 0, 0], [0, 1, 0, 1], [0, 0, 1, 1], [1, 0, 1, 0]], F32)
    place = jnp.arange(2 * elems, dtype=jnp.int32)
    side_hot = (nbr_side[:, :, None] == sides).astype(F32) @ corner
    theirs = (near[:, :, None] == place).astype(F32)[..., None] * side_hot[:, :, None, :]
    home = (jnp.arange(elems, dtype=jnp.int32)[:, None] + elems // 2 == place).astype(F32)
    ours = home[:, None, :, None] * corner[None, :, None, :]
    pick = (0.5 * (theirs + ours)).astype(BF16).reshape(COLS, 2 * COLS)
    return dot(pick, table).reshape(elems, 4, 4 * LEV)


def precip_part(precip, span_map, active):
    spans, rows = 32, 24
    hot = ((span_map[:, None] == jnp.arange(spans, dtype=jnp.int32)) & (active[:, None] > 0)).astype(F32)
    earlier = jnp.cumsum(hot, 0) - hot
    cast = precip[:, None]
    first = jnp.sum(jnp.where(earlier == 0, hot, 0) * cast, 0)
    second = jnp.sum(jnp.where(earlier == 1, hot, 0) * cast, 0)
    sent = jnp.stack([first, second, jnp.sum(hot, 0)], 1)
    got = lax.all_to_all(sent, "span", split_axis=0, concat_axis=0, tiled=True)
    load = got[:, 2]
    start = (jnp.cumsum(load) - load)[:, None]
    place = jnp.arange(rows, dtype=F32)[None, :]
    one = jnp.where((start == place) & (load[:, None] > 0.5), got[:, 0:1], 0.0)
    two = jnp.where((start + 1 == place) & (load[:, None] > 1.5), got[:, 1:2], 0.0)
    return jnp.sum(one + two, 0)


def body(column_state, crm_fields, span_map, active, density, nbr_elem, nbr_side):
    tendency, fresh, precip = crm_call(column_state, crm_fields, active, density)
    edge_sums = edge_part(tendency, nbr_elem, nbr_side)
    span_precip = precip_part(precip[0], span_map, active)
    return (tendency, fresh, span_precip, edge_sums)


def solution(mesh):
    rows = P(("region", "span"), None)
    line = P(("region", "span"))
    return jax.shard_map(
        body,
        mesh=mesh,
        in_specs=(rows, rows, line, line, P(), rows, rows),
        out_specs=(rows, rows, line, P(("region", "span"), None, None)),
        check_vma=False,
    )
```

time: 540 us -> 80.9 us (0.15)
  other arithmetic: 302 us -> 2.66 us
  waiting for transfers between devices: 131 us -> 10 us
  starting transfers between devices: 69.1 us -> 38.5 us
  Pallas kernels: 0 us -> 15.3 us
  matrix products: 8.7 us -> 0.26 us
  local copies, waits for them, and re-layouts: 20.5 us -> 12.5 us
    sub x11 -> x1, other arithmetic: 192 us -> 0.12 us  [precip_part(): start = (jnp.cumsum(load) - load)[:, None]]
    all_to_all x5 -> x1, waiting for transfers between devices: 83.3 us -> 10 us  [precip_part(): got = lax.all_to_all(sent, 'span', split_axis=0, concat_axis=0, tiled=True)]
    unnamed x29 -> x0, other arithmetic: 67 us -> none
    ppermute x2, waiting for transfers between devices: 47.9 us -> 0.01 us  [the longest x1 0.01 us: edge_part(): lax.ppermute(tendency[half:], axes, up)]
    mul x5 -> x1, other arithmetic: 35.3 us -> 0.05 us  [edge_part(): (near[:, :, None] == place).astype(F32)[..., None] * side_hot[:, :, None, :]]
    all_to_all x5 -> x1, starting transfers between devices: 63.1 us -> 28.7 us  [precip_part(): got = lax.all_to_all(sent, 'span', split_axis=0, concat_axis=0, tiled=True)]
    pallas_call x0 -> x1, Pallas kernels: none -> 15.3 us  [crm_call(): pl.pallas_call(crm_kernel, out_shape=(jax.ShapeDtypeStruct((COLS, 4 * LEV...]
    unnamed x292 -> x40, local copies, waits for them, and re-layouts: 2.25 us -> 11.5 us
  transfers between devices with their start and end apart: 7 -> 3, of which waited for: 5 -> 1; matrix products, arithmetic and copies ran while one was open for 39% -> 2% of each run, Pallas kernels for 0% -> 0%
where the time goes in v1:
time: 80.9 us; the launch traced here: 80.1 us
  starting transfers between devices  38.5 us (48%)
  Pallas kernels  15.3 us (19%)
  local copies, waits for them, and re-layouts  12.5 us (15%)
  waiting for transfers between devices  10 us (12%)
  other arithmetic  2.66 us (3%)
  between operations  0.82 us (1%)
    all_to_all x1, starting transfers between devices, precip_part(): got = lax.all_to_all(sent, 'span', split_axis=0, concat_axis=0, tiled=True)  28.7 us
    pallas_call x1, Pallas kernels, crm_call(): pl.pallas_call(crm_kernel, out_shape=(jax.ShapeDtypeStruct((COLS, 4 * LEV...  15.3 us
    unnamed x40, local copies, waits for them, and re-layouts  11.5 us
    all_to_all x1, waiting for transfers between devices, precip_part(): got = lax.all_to_all(sent, 'span', split_axis=0, concat_axis=0, tiled=True)  10 us
    ppermute x1, starting transfers between devices, edge_part(): lax.ppermute(tendency[:half], axes, down)  6.08 us
    ppermute x1, starting transfers between devices, edge_part(): lax.ppermute(tendency[half:], axes, up)  3.7 us
  transfers between devices with their start and end apart: 3, of which 1 were waited for; matrix products, arithmetic and copies ran while one was open for 2% of the time, Pallas kernels for 0%

profile of v1, /device:TPU:6, one launch (start us, length us, event | category | flops | bytes accessed | tf_op | source)
XLA Modules:
  0.0 80.1 jit_solution(5927388544951714182)
XLA Ops:
  0.6 0.7 broadcast_compare_fusion
  1.3 0.7 fusion.11
  2.1 0.1 reduce_window_sum.18
  2.2 0.6 copy-done.10
  2.9 1.1 %copy-done = bf16[64,5568]{1,0:T(8,128)(2,1)S(1)} copy-done((bf16[64,5568]{1,0:T(8,128)(2,1)S(1)}, bf16[64,5568]{1,0:T(8,128)(2,1)}, u32[]{:S(2)}) %copy-start) | copy-done | bytes 712728
  4.0 1.0 %copy-done.1 = f32[288,192]{1,0:T(8,128)S(1)} copy-done((f32[288,192]{1,0:T(8,128)S(1)}, f32[288,192]{1,0:T(8,128)}, u32[]{:S(2)}) %copy-start.1) | copy-done | bytes 221208
  4.9 1.0 %copy-done.2 = bf16[2,192,288]{2,1,0:T(8,128)(2,1)S(1)} copy-done((bf16[2,192,288]{2,1,0:T(8,128)(2,1)S(1)}, bf16[2,192,288]{2,1,0:T(8,128)(2,1)}, u32[]{:S(2)}) %copy-start.2) | copy-done | bytes 221208
  5.9 0.9 %copy-done.3 = bf16[256,512]{1,0:T(8,128)(2,1)S(1)} copy-done((bf16[256,512]{1,0:T(8,128)(2,1)S(1)}, bf16[256,512]{1,0:T(8,128)(2,1)}, u32[]{:S(2)}) %copy-start.3) | copy-done | bytes 262168
  6.9 0.9 %copy-done.4 = bf16[512,256]{1,0:T(8,128)(2,1)S(1)} copy-done((bf16[512,256]{1,0:T(8,128)(2,1)S(1)}, bf16[512,256]{1,0:T(8,128)(2,1)}, u32[]{:S(2)}) %copy-start.4) | copy-done | bytes 262168
  7.8 0.9 %copy-done.5 = bf16[64,928]{1,0:T(8,128)(2,1)S(1)} copy-done((bf16[64,928]{1,0:T(8,128)(2,1)S(1)}, bf16[64,928]{1,0:T(8,128)(2,1)}, u32[]{:S(2)}) %copy-start.5) | copy-done | bytes 118808
  8.7 0.8 %copy-done.7 = bf16[128,256]{1,0:T(8,128)(2,1)S(1)} copy-done((bf16[128,256]{1,0:T(8,128)(2,1)S(1)}, bf16[128,256]{1,0:T(8,128)(2,1)}, u32[]{:S(2)}) %copy-start.7) | copy-done | bytes 65560
  9.5 0.8 copy-done.9
  10.3 15.3 %shard_map.192 = (bf16[64,288]{1,0:T(8,128)(2,1)}, bf16[64,5568]{1,0:T(8,128)(2,1)}, f32[1,64]{1,0:T(1,128)S(1)}) custom-call(bf16[64,288]{1,0:T(8,128)(2,1)S(1)} %copy-done.8, bf16[64,5568]{1,0:T(8,128)(2,1)S(1)} %copy-done, s32[64]{0:T(128)S(1)} %copy-done.12, f32[58]{0:T(128)S(1)} %copy-done.11, f32[1,58]{1,0:T(1,128)S(1)} %bitcast.19, ...), custom_call_target="tpu_custom_call" | custom-call | tf_op jit(solution)/shard_map/pallas_call | solution.py:285
  25.6 0.7 copy-done.14
  26.3 0.1 fusion.7
  26.4 0.7 copy.45
  27.1 28.7 %all-to-all-start = ((f32[32,1,3]{2,1,0:T(1,128)}), f32[32,1,3]{2,1,0:T(1,128)S(1)}, u32[]{:S(2)}, u32[]{:S(2)}) async-start(f32[32,1,3]{2,1,0:T(1,128)} %copy.45), calls=%async_computation | async-start | bytes 32768 | tf_op jit(solution)/shard_map/all_to_all | solution.py:351
  55.9 3.7 %collective-permute-start = (bf16[32,288]{1,0:T(8,128)(2,1)S(1)}, bf16[32,288]{1,0:T(8,128)(2,1)S(1)}, u32[]{:S(2)}, u32[]{:S(2)}) collective-permute-start(bf16[32,288]{1,0:T(8,128)(2,1)S(1)} %get-tuple-element.37), channel_id=1, source_target_pairs={{0,1},{1,2},{2,3},{3,4},{4,5},{5,6},{6,7},{7,8},{8,9},{9,10},{10,1... | collective-permute-start | bytes 55304 | tf_op jit(solution)/shard_map/ppermute | solution.py:323
  59.6 6.1 %collective-permute-start.1 = (bf16[32,288]{1,0:T(8,128)(2,1)S(1)}, bf16[32,288]{1,0:T(8,128)(2,1)S(1)}, u32[]{:S(2)}, u32[]{:S(2)}) collective-permute-start(bf16[32,288]{1,0:T(8,128)(2,1)S(1)} %get-tuple-element.38), channel_id=1, source_target_pairs={{1,0},{2,1},{3,2},{4,3},{5,4},{6,5},{7,6},{8,7},{9,8},{10,9},{11,1... | collective-permute-start | bytes 55304 | tf_op jit(solution)/shard_map/ppermute | solution.py:325
  65.7 0.7 copy-done.16
  66.4 0.6 copy-done.17
  67.1 0.1 fusion.18
  67.3 0.6 copy-done.15
  68.0 0.1 mul.85
  68.1 0.1 copy.50
  68.2 10.0 %all-to-all-done = f32[32,1,3]{2,1,0:T(1,128)S(1)} async-done(((f32[32,1,3]{2,1,0:T(1,128)}), f32[32,1,3]{2,1,0:T(1,128)S(1)}, u32[]{:S(2)}, u32[]{:S(2)}) %all-to-all-start) | async-done | bytes 416 | tf_op jit(solution)/shard_map/all_to_all | solution.py:351
  78.3 0.1 copy.55
  78.4 0.1 compare_reduce_fusion.1
  78.5 0.1 subtract_reduce_fusion
  78.7 0.6 add_reduce_fusion.1
  79.3 0.1 fusion
  79.5 0.7 copy.52
  (40 shorter events, 0.5 us)
Async XLA Ops:
  0.6 1.6 %copy-start.6 = (bf16[256,128]{1,0:T(8,128)(2,1)S(1)}, bf16[256,128]{1,0:T(8,128)(2,1)}, u32[]{:S(2)}) copy-start(bf16[256,128]{1,0:T(8,128)(2,1)} %constant.78.clone.gather_ref) | copy-start | bytes 196612
  1.3 0.9 %copy-start.8 = (bf16[64,288]{1,0:T(8,128)(2,1)S(1)}, bf16[64,288]{1,0:T(8,128)(2,1)}, u32[]{:S(2)}) copy-start(bf16[64,288]{1,0:T(8,128)(2,1)} %state_ref.1) | copy-start | bytes 110596
  2.1 0.7 copy-start.10
  2.2 0.7 copy-start.11
  2.2 0.7 copy-start.12
  2.9 1.1 %copy-start = (bf16[64,5568]{1,0:T(8,128)(2,1)S(1)}, bf16[64,5568]{1,0:T(8,128)(2,1)}, u32[]{:S(2)}) copy-start(bf16[64,5568]{1,0:T(8,128)(2,1)} %fields_ref.1) | copy-start | bytes 2138116
  4.0 1.0 %copy-start.1 = (f32[288,192]{1,0:T(8,128)S(1)}, f32[288,192]{1,0:T(8,128)}, u32[]{:S(2)}) copy-start(f32[288,192]{1,0:T(8,128)} %constant.80.clone.fall_ref) | copy-start | bytes 663556
  4.9 1.0 %copy-start.2 = (bf16[2,192,288]{2,1,0:T(8,128)(2,1)S(1)}, bf16[2,192,288]{2,1,0:T(8,128)(2,1)}, u32[]{:S(2)}) copy-start(bf16[2,192,288]{2,1,0:T(8,128)(2,1)} %constant.76.clone.rise_ref) | copy-start | bytes 663556
  5.9 0.9 %copy-start.3 = (bf16[256,512]{1,0:T(8,128)(2,1)S(1)}, bf16[256,512]{1,0:T(8,128)(2,1)}, u32[]{:S(2)}) copy-start(bf16[256,512]{1,0:T(8,128)(2,1)} %constant.74.clone.back_ref) | copy-start | bytes 786436
  6.9 0.9 %copy-start.4 = (bf16[512,256]{1,0:T(8,128)(2,1)S(1)}, bf16[512,256]{1,0:T(8,128)(2,1)}, u32[]{:S(2)}) copy-start(bf16[512,256]{1,0:T(8,128)(2,1)} %constant.73.clone.forward_ref) | copy-start | bytes 786436
  7.8 0.9 %copy-start.5 = (bf16[64,928]{1,0:T(8,128)(2,1)S(1)}, bf16[64,928]{1,0:T(8,128)(2,1)}, u32[]{:S(2)}) copy-start(bf16[64,928]{1,0:T(8,128)(2,1)} %constant.79.clone.tally_ref) | copy-start | bytes 356356
  8.7 0.8 %copy-start.7 = (bf16[128,256]{1,0:T(8,128)(2,1)S(1)}, bf16[128,256]{1,0:T(8,128)(2,1)}, u32[]{:S(2)}) copy-start(bf16[128,256]{1,0:T(8,128)(2,1)} %constant.72.clone.dxm_ref) | copy-start | bytes 196612
  9.5 0.8 copy-start.9
  25.6 0.7 copy-start.14
  26.3 29.6 %copy-start.13 = (bf16[64,288]{1,0:T(8,128)(2,1)S(1)}, bf16[64,288]{1,0:T(8,128)(2,1)}, u32[]{:S(2)}) copy-start(bf16[64,288]{1,0:T(8,128)(2,1)} %get-tuple-element.26) | copy-start | bytes 110596
  27.1 51.1 %all-to-all-start = ((f32[32,1,3]{2,1,0:T(1,128)}), f32[32,1,3]{2,1,0:T(1,128)S(1)}, u32[]{:S(2)}, u32[]{:S(2)}) async-start(f32[32,1,3]{2,1,0:T(1,128)} %copy.45), calls=%async_computation | async-start | bytes 32768 | tf_op jit(solution)/shard_map/all_to_all | solution.py:351
  55.9 23.5 %collective-permute-start = (bf16[32,288]{1,0:T(8,128)(2,1)S(1)}, bf16[32,288]{1,0:T(8,128)(2,1)S(1)}, u32[]{:S(2)}, u32[]{:S(2)}) collective-permute-start(bf16[32,288]{1,0:T(8,128)(2,1)S(1)} %get-tuple-element.37), channel_id=1, source_target_pairs={{0,1},{1,2},{2,3},{3,4},{4,5},{5,6},{6,7},{7,8},{8,9},{9,10},{10,1... | collective-permute-start | bytes 55304 | tf_op jit(solution)/shard_map/ppermute | solution.py:323
  59.6 19.8 %collective-permute-start.1 = (bf16[32,288]{1,0:T(8,128)(2,1)S(1)}, bf16[32,288]{1,0:T(8,128)(2,1)S(1)}, u32[]{:S(2)}, u32[]{:S(2)}) collective-permute-start(bf16[32,288]{1,0:T(8,128)(2,1)S(1)} %get-tuple-element.38), channel_id=1, source_target_pairs={{1,0},{2,1},{3,2},{4,3},{5,4},{6,5},{7,6},{8,7},{9,8},{10,9},{11,1... | collective-permute-start | bytes 55304 | tf_op jit(solution)/shard_map/ppermute | solution.py:325
  65.7 0.7 copy-start.16
  66.4 0.7 copy-start.17
  66.4 0.7 copy-start.18
  67.3 0.7 copy-start.15

commit v2 on v1

v2 whole, which is shorter than its diff:
```python
import functools

import jax
import jax.numpy as jnp
import ml_dtypes
import numpy as np
from jax import lax
from jax.experimental import pallas as pl
from jax.experimental.pallas import tpu as pltpu
from jax.sharding import PartitionSpec as P

HIGH = lax.Precision.HIGHEST
MESH = pl.DeviceIdType.MESH
LEV, NZ, NX, COLS = 72, 58, 32, 64
G, R, LANES = 4, 16, 128
ROWS = NZ * R
WIDE, CHUNKS = 512, 11
F32, BF16 = jnp.float32, jnp.bfloat16


def split(a):
    high = a.astype(ml_dtypes.bfloat16)
    return high, (a - high.astype(np.float64)).astype(ml_dtypes.bfloat16)


def level_map(count_to, count_from):
    index = np.arange(count_to)
    numerator = (2 * index + 1) * count_from - count_to
    lower = np.clip(numerator // (2 * count_to), 0, count_from - 2)
    fraction = np.clip((numerator - lower * 2 * count_to) / (2 * count_to), 0.0, 1.0)
    target = np.arange(count_from)[None, :]
    return (1 - fraction)[:, None] * (target == lower[:, None]) + fraction[:, None] * (
        target == lower[:, None] + 1
    )


@functools.cache
def tables():
    eye = np.eye(G)
    step = 0.5 * (np.roll(np.eye(NX), 1, 0) - np.roll(np.eye(NX), -1, 0))
    dxm = np.concatenate(
        [np.kron(eye, 0.25 * step), np.kron(eye, np.full((NX, NX), 0.25 / NX))], 1
    ).astype(ml_dtypes.bfloat16)
    mode = np.arange(NX)
    wave = np.where(mode <= NX // 2, mode, mode - NX // 2)
    phase = 2 * np.pi * (wave[:, None] * np.arange(NX)[None, :] % NX) / NX
    norm = np.where((mode == 0) | (mode == NX // 2), np.sqrt(1 / NX), np.sqrt(2 / NX))
    four = norm[:, None] * np.where((mode <= NX // 2)[:, None], np.cos(phase), np.sin(phase))
    eigen = np.tile(2 - 2 * np.cos(2 * np.pi * wave / NX), G)[None, :]
    eigen = np.broadcast_to(eigen, (R, LANES)).astype(np.float32)

    def doubled(a):
        return np.concatenate(split(a), 1)

    to_mode = -four.T
    forward = np.concatenate(
        [doubled(np.kron(eye, a)) for a in (step @ to_mode, step @ to_mode, to_mode, to_mode)], 0
    )
    back = np.concatenate([np.kron(eye, 0.5 * four), np.kron(eye, four @ step)], 1)
    back = np.concatenate([doubled(back)] * 2, 0)
    up = level_map(NZ, LEV)
    zero = np.zeros_like(up)
    blocks = [
        [0.3 * up, zero, zero, zero],
        [zero, 0.25 * up, zero, 0.25 * up],
        [zero, zero, 0.25 * up, zero],
    ]
    rise = np.zeros((192, 4 * LEV))
    for i, row in enumerate(blocks):
        rise[64 * i : 64 * i + NZ] = np.concatenate(row, 1)
    rise = np.stack(split(rise))
    column, lane = np.arange(LANES) % COLS, np.arange(LANES)
    spread = (column[:, None] // R == lane[None, :] // NX).astype(ml_dtypes.bfloat16)
    gather = (lane[:, None] // NX == column[None, :] // R) / NX
    gather = np.concatenate([gather, gather], 0).astype(ml_dtypes.bfloat16)
    tally = np.zeros((64, ROWS))
    for z in range(NZ):
        tally[z, R * z : R * z + R] = 1
    tally = tally.astype(ml_dtypes.bfloat16)
    down = level_map(LEV, NZ)
    fall = np.zeros((4 * LEV, 192))
    for f, (source, gain) in enumerate(((0, 2.0), (1, 4.0), (2, 4.0), (0, 0.5))):
        fall[LEV * f : LEV * f + LEV, 64 * source : 64 * source + NZ] = gain * down
    fall = np.stack(split(fall.T))
    return dxm, forward, back, eigen, rise, spread, gather, tally, fall


def dot(a, b, dims=((1,), (0,)), precision=None):
    return lax.dot_general(a, b, (dims, ((), ())), precision=precision, preferred_element_type=F32)


def halves(a):
    high = a.astype(BF16)
    return high, (a - high.astype(F32)).astype(BF16)


def regroup(parts):
    lane = lax.broadcasted_iota(jnp.int32, (R, LANES), 1)
    low, even = lane < 64, (lane & 32) == 0
    a, b, c, d = parts
    a, c = jnp.where(low, a, pltpu.roll(c, 64, 1)), jnp.where(low, pltpu.roll(a, 64, 1), c)
    b, d = jnp.where(low, b, pltpu.roll(d, 64, 1)), jnp.where(low, pltpu.roll(b, 64, 1), d)
    a, b = jnp.where(even, a, pltpu.roll(b, 32, 1)), jnp.where(even, pltpu.roll(a, 96, 1), b)
    c, d = jnp.where(even, c, pltpu.roll(d, 32, 1)), jnp.where(even, pltpu.roll(c, 96, 1), d)
    return a, b, c, d


def crm_kernel(
    state_hbm, fields_hbm, active_hbm, density_hbm,
    dxm_hbm, forward_hbm, back_hbm, eigen_hbm, rise_hbm, spread_hbm, gather_hbm, tally_hbm, fall_hbm,
    tend_hbm, fresh_hbm, precip_hbm,
    state_ref, fields_ref, active_ref, density_ref, density_row_ref,
    dxm_ref, forward_ref, back_ref, eigen_ref, rise_ref, spread_ref, gather_ref, tally_ref, fall_ref,
    tend_ref, fresh_ref, precip_ref,
    raw, dxm, prof_wide, prof_rows, inv, coup, u1, w1, left, sol, cells, pres, means, fresh,
    in_sem, field_sem, out_sem, fresh_sem,
):
    copies = {}
    pairs = dict(
        state=(state_hbm, state_ref), rise=(rise_hbm, rise_ref), active=(active_hbm, active_ref),
        spread=(spread_hbm, spread_ref), dxm=(dxm_hbm, dxm_ref), density=(density_hbm, density_ref),
        eigen=(eigen_hbm, eigen_ref), forward=(forward_hbm, forward_ref), back=(back_hbm, back_ref),
        gather=(gather_hbm, gather_ref), tally=(tally_hbm, tally_ref), fall=(fall_hbm, fall_ref),
        density_row=(density_hbm, density_row_ref),
    )
    for n, (name, (source, target)) in enumerate(pairs.items()):
        copies[name] = pltpu.make_async_copy(source, target, in_sem.at[n])
        if n == 6:
            for k in range(CHUNKS):
                cut = slice(WIDE * k, min(WIDE * k + WIDE, NZ * NX * 3))
                copies[k] = pltpu.make_async_copy(
                    fields_hbm.at[:, cut], fields_ref.at[:, cut], field_sem.at[k]
                )
                copies[k].start()
        copies[name].start()

    lane = lax.broadcasted_iota(jnp.int32, (R, LANES), 1)
    row = lax.broadcasted_iota(jnp.int32, (R, LANES), 0)
    own = (lane & (R - 1)) == row
    zero16 = jnp.zeros((R, LANES), BF16)

    copies["state"].wait()
    copies["rise"].wait()
    copies["active"].wait()
    state = state_ref[...]
    profile = dot(rise_ref[0], state, ((1,), (1,))) + dot(rise_ref[1], state, ((1,), (1,)))
    flags = active_ref[...].reshape(1, COLS).astype(F32)
    p_high, p_low = halves(jnp.concatenate([jnp.exp(profile[:64]), profile[64:]], 0))
    prof_wide[...] = jnp.concatenate([p_high, p_low], 1).astype(F32)
    keep = jnp.concatenate([flags, flags], 1)
    prof_wide[63:64] = jnp.where(lane[:1] < COLS, keep, 0.0)
    wanted = [64 * f + z for f in range(3) for z in range(NZ)] + [63]
    for k in range(0, len(wanted), 8):
        lines = [prof_wide[i : i + 1] for i in wanted[k : k + 8]]
        lines = [jnp.where(own, jnp.broadcast_to(v, (R, LANES)), 0.0).astype(BF16) for v in lines]
        for i, v in zip(wanted[k : k + 8], lines):
            prof_rows[i] = v
    copies["spread"].wait()
    for f in range(3):
        top = 64 if f == 0 else NZ
        block = dot(prof_rows[64 * f : 64 * f + top].reshape(top * R, LANES), spread_ref[...])
        means[f, :top] = block.reshape(top, R, LANES)
    mask = means[0, 63] > 0.5

    for f in range(3):
        raw[f, 0] = zero16
        raw[f, NZ + 1] = zero16
    for k in range(CHUNKS):
        copies[k].wait()
        blocks = []
        for j in range(4 * k, 4 * k + 4):
            if j < 43:
                tiles = [fields_ref[R * g : R * g + R, LANES * j : LANES * j + LANES] for g in range(G)]
            else:
                tiles = [
                    jnp.concatenate([fields_ref[R * g : R * g + R, LANES * j :], zero16[:, :64]], 1)
                    for g in range(G)
                ]
            blocks.append(regroup(tiles))
        for j, block in enumerate(blocks):
            for part, level in zip(block, range(16 * k + 4 * j, min(16 * k + 4 * j + 4, 3 * NZ))):
                f, z = divmod(level, NZ)
                raw[f, z + 1] = part
    copies["dxm"].wait()
    for f in range(3):
        block = dot(raw[f, 1 : NZ + 1].reshape(ROWS, LANES), dxm_ref[...])
        dxm[f] = block.reshape(NZ, R, 2 * LANES)

    copies["density"].wait()
    copies["eigen"].wait()
    eigen = eigen_ref[...]
    inv[0] = jnp.zeros((R, LANES), F32)
    zero = inv[0]

    def factor(t, last):
        low, high, _ = last
        z = NZ - 1 - t
        rho, above = density_ref[t], density_ref[t + 1]
        below = jnp.where(t > 0, density_ref[jnp.maximum(t - 1, 0)], rho)
        f_up, f_down = 0.5 * (rho + above), 0.5 * (rho + below)
        i_low = 1.0 / ((eigen * rho + (f_up + f_down)) - f_down * low)
        e_low = f_up * i_low
        rho, below = density_ref[z], density_ref[z - 1]
        above = jnp.where(t > 0, density_ref[jnp.minimum(z + 1, NZ - 1)], rho)
        f_up, f_down = 0.5 * (rho + above), 0.5 * (rho + below)
        diag = (eigen * rho + (f_up + f_down)) - f_up * high
        i_high = 1.0 / diag
        e_high = f_down * i_high
        stores = [(inv, t, i_low), (coup, t, e_low), (inv, z, i_high), (coup, z, e_high)]
        return stores, (e_low, e_high, diag)

    def advect(z, carry):
        (u_m, u), (w_m, w), (q_m, q), (rw_mm, rw_m) = carry
        u_p, w_p, q_p = [raw[f, z + 2].astype(F32) for f in range(3)]
        rho = density_ref[z]
        half = 0.125 * w
        du, mean_u = dxm[0, z, :, :LANES], dxm[0, z, :, LANES:]
        dw = dxm[1, z, :, :LANES]
        dq, mean_q = dxm[2, z, :, :LANES], dxm[2, z, :, LANES:]
        new_u = u - u * du - half * (u_p - u_m) + (means[2, z] - mean_u)
        new_w = w - u * dw - half * (w_p - w_m) + (0.125 * q - 0.5 * mean_q)
        new_q = q - u * dq - half * (q_p - q_m) + (means[1, z] - mean_q)
        x = new_q - means[0, z]
        cond = jnp.maximum(x, 0.0) + jnp.log(1.0 + jnp.exp(-jnp.abs(x)))
        q2 = new_q - 0.5 * cond
        rw = rho * new_w
        stores = [
            (u1, z, new_u),
            (w1, z, new_w),
            (fresh, 2 * NZ + z, jnp.where(mask, q2, q).astype(BF16)),
            (cells.at[0], z, jnp.concatenate(halves(cond), 1)),
            (cells.at[1], z, jnp.concatenate(halves(q2 - q), 1)),
            (left.at[:, :, : 2 * LANES], z + 1, jnp.concatenate(halves(rho * new_u), 1)),
            (left.at[:, :, 2 * LANES :], z, jnp.concatenate(halves(0.5 * (rw - rw_mm)), 1)),
        ]
        return stores, ((u, u_p), (w, w_p), (q, q_p), (rw_m, rw))

    def both_passes(t, carry):
        stores, last = factor(t, carry[0])
        more, levels = advect(2 * t, carry[1])
        most, levels = advect(2 * t + 1, levels)
        for ref, z, value in stores + more + most:
            ref[z] = value
        return last, levels

    first = tuple((zero, raw[f, 1].astype(F32)) for f in range(3)) + ((zero, zero),)
    last, levels = lax.fori_loop(0, NZ // 2, both_passes, ((zero, zero, zero), first))
    left[NZ, :, 2 * LANES :] = jnp.concatenate(halves(-0.5 * levels[3][0]), 1)
    mid = NZ // 2
    centre = 1.0 / (last[2] - 0.5 * (density_ref[mid - 1] + density_ref[mid]) * last[0])

    def give_back(k):
        blocks = []
        for j in range(4 * k, 4 * k + 4):
            blocks.append(
                regroup([fresh[v] if v < 3 * NZ else zero16 for v in range(4 * j, 4 * j + 4)])
            )
        for j, block in enumerate(blocks):
            j += 4 * k
            for g, part in enumerate(block):
                if j < 43:
                    fresh_ref[R * g : R * g + R, LANES * j : LANES * j + LANES] = part
                else:
                    fresh_ref[R * g : R * g + R, LANES * j :] = part[:, :64]
        cut = slice(WIDE * k, min(WIDE * k + WIDE, NZ * NX * 3))
        copy = pltpu.make_async_copy(fresh_ref.at[:, cut], fresh_hbm.at[:, cut], fresh_sem.at[k])
        copy.start()
        return copy

    leaving = [give_back(k) for k in range(8, CHUNKS)]

    copies["forward"].wait()
    right = dot(left[1:].reshape(ROWS, 4 * LANES), forward_ref[...])
    sol[...] = (right[:, :LANES] + right[:, LANES:]).reshape(NZ, R, LANES)
    low, high = sol[0], sol[NZ - 1]
    for t in range(1, mid):
        z = NZ - 1 - t
        low = sol[t] + coup[t - 1] * low
        high = sol[z] + coup[z + 1] * high
        sol[t], sol[z] = low, high
    high = centre * (high + coup[mid - 1] * low)
    low = inv[mid - 1] * low + coup[mid - 1] * high
    left[mid - 1, :, : 2 * LANES] = jnp.concatenate(halves(low), 1)
    left[mid, :, : 2 * LANES] = jnp.concatenate(halves(high), 1)
    for t in range(mid - 2, -1, -1):
        z = NZ - 1 - t
        low = inv[t] * sol[t] + coup[t] * low
        high = inv[z] * sol[z] + coup[z] * high
        left[t, :, : 2 * LANES] = jnp.concatenate(halves(low), 1)
        left[z, :, : 2 * LANES] = jnp.concatenate(halves(high), 1)
    copies["back"].wait()
    both = dot(left[:NZ, :, : 2 * LANES].reshape(ROWS, 2 * LANES), back_ref[...])
    pres[0] = zero
    pres[NZ + 1] = zero
    pres[1 : NZ + 1] = (both[:, :LANES] + both[:, 2 * LANES : 3 * LANES]).reshape(NZ, R, LANES)
    sol[...] = (both[:, LANES : 2 * LANES] + both[:, 3 * LANES :]).reshape(NZ, R, LANES)

    @pl.loop(0, NZ // 2)
    def _(t):
        z = 2 * t
        here = pl.ds(z, 2)
        u, w = raw[0, pl.ds(z + 1, 2)].astype(F32), raw[1, pl.ds(z + 1, 2)].astype(F32)
        u2 = u1[here] - sol[here]
        w2 = w1[here] - (pres[pl.ds(z + 2, 2)] - pres[here])
        u_out = jnp.where(mask[None], u2, u).astype(BF16)
        w_out = jnp.where(mask[None], w2, w).astype(BF16)
        change = jnp.concatenate(halves(u2 - u), 2)
        fresh[here] = u_out
        fresh[pl.ds(NZ + z, 2)] = w_out
        cells[2, here] = change

    copies["gather"].wait()
    for f in range(3):
        total = dot(cells[f].reshape(ROWS, 2 * LANES), gather_ref[...])
        means[f, :NZ] = total.reshape(NZ, R, LANES)
    lane_high = lane < COLS

    @pl.loop(0, NZ // 2)
    def _(t):
        here = pl.ds(2 * t, 2)
        values = []
        for f in range(3):
            value = jnp.where(own[None], means[f, here], 0.0)
            high = value.astype(BF16).astype(F32)
            values.append(jnp.where(lane_high[None], high, value - high).astype(BF16))
        left[here, :, : 3 * LANES] = jnp.concatenate(values, 2)

    copies["tally"].wait()
    total = dot(tally_ref[...], left[:NZ, :, : 3 * LANES].reshape(ROWS, 3 * LANES))
    copies["density_row"].wait()
    weights = density_row_ref[...].reshape(1, NZ) * (2.0 / NZ)
    precip = dot(weights, total[:NZ, :LANES], precision=HIGH)
    precip_ref[...] = precip[:, :COLS] + precip[:, COLS:]
    total = jnp.concatenate([total[:, LANES * f : LANES * f + LANES] for f in range(3)], 0)
    t_high, t_low = halves(jnp.where(keep > 0.5, total, 0.0).T)
    copies["fall"].wait()
    tend = dot(t_high, fall_ref[0]) + dot(t_low, fall_ref[0]) + dot(t_high, fall_ref[1])
    tend_ref[...] = (tend[:COLS] + tend[COLS:]).astype(BF16)
    leaving.append(pltpu.make_async_copy(tend_ref, tend_hbm, out_sem.at[0]))
    leaving[-1].start()
    leaving.append(pltpu.make_async_copy(precip_ref, precip_hbm, out_sem.at[1]))
    leaving[-1].start()
    leaving += [give_back(k) for k in range(8)]
    for copy in leaving:
        copy.wait()


def crm_call(column_state, crm_fields, active, density):
    constants = [jnp.asarray(a) for a in tables()]
    hbm = pl.BlockSpec(memory_space=pltpu.HBM)
    levels = (NZ, R, LANES)
    return pl.pallas_call(
        crm_kernel,
        out_shape=(
            jax.ShapeDtypeStruct((COLS, 4 * LEV), BF16),
            jax.ShapeDtypeStruct((COLS, 3 * NZ * NX), BF16),
            jax.ShapeDtypeStruct((1, COLS), F32),
        ),
        in_specs=[hbm] * (4 + len(constants)),
        out_specs=(hbm, hbm, hbm),
        scratch_shapes=[
            pltpu.VMEM((COLS, 4 * LEV), BF16),
            pltpu.VMEM((COLS, 3 * NZ * NX), BF16),
            pltpu.VMEM((COLS,), jnp.int32),
            pltpu.SMEM((NZ,), F32),
            pltpu.VMEM((NZ,), F32),
            *[pltpu.VMEM(a.shape, a.dtype) for a in constants],
            pltpu.VMEM((COLS, 4 * LEV), BF16),
            pltpu.VMEM((COLS, 3 * NZ * NX), BF16),
            pltpu.VMEM((1, COLS), F32),
            pltpu.VMEM((3, NZ + 2, R, LANES), BF16),
            pltpu.VMEM((3, NZ, R, 2 * LANES), F32),
            pltpu.VMEM((192, LANES), F32),
            pltpu.VMEM((192, R, LANES), BF16),
            pltpu.VMEM(levels, F32),
            pltpu.VMEM(levels, F32),
            pltpu.VMEM(levels, F32),
            pltpu.VMEM(levels, F32),
            pltpu.VMEM((NZ + 1, R, 4 * LANES), BF16),
            pltpu.VMEM(levels, F32),
            pltpu.VMEM((3, NZ, R, 2 * LANES), BF16),
            pltpu.VMEM((NZ + 2, R, LANES), F32),
            pltpu.VMEM((3, 64, R, LANES), F32),
            pltpu.VMEM((3 * NZ, R, LANES), BF16),
            pltpu.SemaphoreType.DMA((13,)),
            pltpu.SemaphoreType.DMA((CHUNKS,)),
            pltpu.SemaphoreType.DMA((2,)),
            pltpu.SemaphoreType.DMA((CHUNKS,)),
        ],
        compiler_params=pltpu.CompilerParams(vmem_limit_bytes=63 * 2**20),
    )(column_state, crm_fields, active, density, *constants)


def exchange_kernel(
    shape, tend_ref, precip_ref, span_map_ref, active_ref, nbr_elem_ref, nbr_side_ref,
    edge_ref, rows_ref,
    from_left, from_right, sent, got, flat, send_sem, recv_sem, halo_send, halo_recv,
):
    regions, spans = shape
    region, span = lax.axis_index("region"), lax.axis_index("span")
    me = region * spans + span
    total = regions * spans
    right, left = lax.rem(me + 1, total), lax.rem(me + total - 1, total)
    right, left = (lax.div(right, spans), lax.rem(right, spans)), (lax.div(left, spans), lax.rem(left, spans))

    barrier = pltpu.get_barrier_semaphore()

    def greet(i, _):
        pl.semaphore_signal(
            barrier, inc=1, device_id=(region, lax.rem(span + i, spans)), device_id_type=MESH
        )
        return _

    lax.fori_loop(1, spans, greet, 0)
    for other in (left, right):
        pl.semaphore_signal(barrier, inc=1, device_id=other, device_id_type=MESH)

    target = lax.broadcasted_iota(jnp.int32, (spans, COLS), 0)
    hot = jnp.where(
        (span_map_ref[...].reshape(1, COLS) == target) & (active_ref[...].reshape(1, COLS) > 0), 1.0, 0.0
    )
    upper = lax.broadcasted_iota(jnp.int32, (COLS, COLS), 0) < lax.broadcasted_iota(jnp.int32, (COLS, COLS), 1)
    before = dot(hot.astype(BF16), jnp.where(upper, 1.0, 0.0).astype(BF16))
    precip = precip_ref[...]
    one = jnp.sum(jnp.where(before < 0.5, hot, 0.0) * precip, 1, keepdims=True)
    two = jnp.sum(jnp.where(before > 0.5, hot, 0.0) * precip, 1, keepdims=True)
    load = jnp.sum(hot, 1, keepdims=True)
    lane = lax.broadcasted_iota(jnp.int32, (spans, LANES), 1)
    block = jnp.where(lane == 0, one, jnp.where(lane == 1, two, jnp.where(lane == 2, load, 0.0)))
    for i in range(spans):
        sent[i] = block[i : i + 1]
    got[span] = sent[span]

    pl.semaphore_wait(barrier, spans + 1)
    half = COLS // 2
    halos = [
        pltpu.make_async_remote_copy(
            src_ref=tend_ref.at[part], dst_ref=place, send_sem=halo_send.at[n], recv_sem=halo_recv.at[n],
            device_id=other, device_id_type=MESH,
        )
        for n, (part, place, other) in enumerate(
            ((pl.ds(half, half), from_left, right), (pl.ds(0, half), from_right, left))
        )
    ]
    for halo in halos:
        halo.start()

    def give(i, _):
        there = lax.rem(span + i, spans)
        pltpu.make_async_remote_copy(
            src_ref=sent.at[there], dst_ref=got.at[span], send_sem=send_sem, recv_sem=recv_sem,
            device_id=(region, there), device_id_type=MESH,
        ).start()
        return _

    lax.fori_loop(1, spans, give, 0)

    cell = lax.broadcasted_iota(jnp.int32, (COLS // 4, 2 * COLS), 1)
    elem, corner = cell >> 2, cell & 3
    c_low, c_high = corner & 1, corner >> 1
    home = lax.broadcasted_iota(jnp.int32, (COLS // 4, 2 * COLS), 0) + COLS // 8
    faces = (1 - c_high, c_low, c_high, 1 - c_low)
    everyone = total * (COLS // 4)
    picks = []
    for side in range(4):
        near = nbr_elem_ref[:, side : side + 1] - (me * (COLS // 4) - COLS // 8)
        near = jnp.where(near < 0, near + everyone, near)
        near = jnp.where(near >= everyone, near - everyone, near)
        theirs = nbr_side_ref[:, side : side + 1]
        face = jnp.where(
            theirs < 2, jnp.where(theirs == 0, faces[0], faces[1]), jnp.where(theirs == 2, faces[2], faces[3])
        )
        pick = jnp.where(near == elem, face, 0) + jnp.where(home == elem, faces[side], 0)
        picks.append((0.5 * pick.astype(F32)).astype(BF16))

    for halo in halos:
        halo.wait()
    own = tend_ref[...]
    table = jnp.concatenate([from_left[...], own, from_right[...]], 0)
    for side in range(4):
        edge_ref[:, side, :] = dot(picks[side], table)

    others = pl.ds(0, spans - 1)
    pltpu.make_async_copy(got.at[others], got.at[others], recv_sem).wait()
    for i in range(spans):
        flat[i : i + 1] = got[i]
    table = flat[...]
    lower = lax.broadcasted_iota(jnp.int32, (spans, spans), 0) > lax.broadcasted_iota(jnp.int32, (spans, spans), 1)
    load = table[:, 2:3]
    start = dot(
        jnp.where(lower, 1.0, 0.0).astype(BF16), jnp.broadcast_to(load, (spans, LANES)).astype(BF16)
    )
    place = lane.astype(F32)
    rows = jnp.where((start == place) & (load > 0.5), table[:, 0:1], 0.0)
    rows += jnp.where((start + 1.0 == place) & (load > 1.5), table[:, 1:2], 0.0)
    rows_ref[...] = jnp.sum(rows, 0, keepdims=True)[:, : rows_ref.shape[1]]
    pltpu.make_async_copy(sent.at[others], sent.at[others], send_sem).wait()


def exchange_call(shape, slots, tendency, precip, span_map, active, nbr_elem, nbr_side):
    spans = shape[1]
    vmem = pl.BlockSpec(memory_space=pltpu.VMEM)
    return pl.pallas_call(
        functools.partial(exchange_kernel, shape),
        out_shape=(
            jax.ShapeDtypeStruct((COLS // 4, 4, 4 * LEV), F32),
            jax.ShapeDtypeStruct((1, slots), F32),
        ),
        in_specs=[vmem] * 6,
        out_specs=(vmem, vmem),
        scratch_shapes=[
            pltpu.VMEM((COLS // 2, 4 * LEV), BF16),
            pltpu.VMEM((COLS // 2, 4 * LEV), BF16),
            pltpu.VMEM((spans, 1, LANES), F32),
            pltpu.VMEM((spans, 1, LANES), F32),
            pltpu.VMEM((spans, LANES), F32),
            pltpu.SemaphoreType.DMA,
            pltpu.SemaphoreType.DMA,
            pltpu.SemaphoreType.DMA((2,)),
            pltpu.SemaphoreType.DMA((2,)),
        ],
        compiler_params=pltpu.CompilerParams(
            collective_id=0, has_side_effects=True, vmem_limit_bytes=16 * 2**20
        ),
    )(tendency, precip, span_map, active, nbr_elem, nbr_side)


def body(shape, column_state, crm_fields, span_map, active, density, nbr_elem, nbr_side):
    tendency, fresh, precip = crm_call(column_state, crm_fields, active, density)
    edge_sums, rows = exchange_call(
        shape, COLS * 3 // 8, tendency, precip, span_map, active, nbr_elem, nbr_side
    )
    return (tendency, fresh, rows[0], edge_sums)


def solution(mesh):
    rows = P(("region", "span"), None)
    line = P(("region", "span"))
    return jax.shard_map(
        functools.partial(body, (mesh.shape["region"], mesh.shape["span"])),
        mesh=mesh,
        in_specs=(rows, rows, line, line, P(), rows, rows),
        out_specs=(rows, rows, line, P(("region", "span"), None, None)),
        check_vma=False,
    )
```

time: 80.9 us -> 53.7 us (0.66)
  starting transfers between devices: 38.5 us -> 0 us
  Pallas kernels: 15.3 us -> 49.3 us
  waiting for transfers between devices: 10 us -> 0 us
  local copies, waits for them, and re-layouts: 12.5 us -> 3.47 us
  other arithmetic: 2.66 us -> 0 us
    pallas_call x0 -> x1, Pallas kernels: none -> 37.6 us  [exchange_call(): pl.pallas_call(functools.partial(exchange_kernel, shape), out_shape=(jax....]
    all_to_all x1 -> x0, starting transfers between devices: 28.7 us -> none  [precip_part(): got = lax.all_to_all(sent, 'span', split_axis=0, concat_axis=0, tiled=True)]
    all_to_all x1 -> x0, waiting for transfers between devices: 10 us -> none  [precip_part(): got = lax.all_to_all(sent, 'span', split_axis=0, concat_axis=0, tiled=True)]
    ppermute x2 -> x0, starting transfers between devices: 9.78 us -> none  [the longest x1 6.08 us: edge_part(): lax.ppermute(tendency[:half], axes, down)]
    unnamed x40 -> x14, local copies, waits for them, and re-layouts: 11.5 us -> 3.47 us
    pallas_call x1, Pallas kernels: 15.3 us -> 11.7 us  [crm_call(): pl.pallas_call(crm_kernel, out_shape=(jax.ShapeDtypeStruct((COLS, 4 * LEV...]
  transfers between devices with their start and end apart: 3 -> 0, of which waited for: 1 -> 0; matrix products, arithmetic and copies ran while one was open for 2% -> 0% of each run, Pallas kernels for 0% -> 0%
where the time goes in v2:
time: 53.7 us; the launch traced here: 53.5 us
  Pallas kernels  49.3 us (92%)
  local copies, waits for them, and re-layouts  3.47 us (6%)
  between operations  0.68 us (1%)
    pallas_call x1, Pallas kernels, exchange_call(): pl.pallas_call(functools.partial(exchange_kernel, shape), out_shape=(jax....  37.6 us
    pallas_call x1, Pallas kernels, crm_call(): pl.pallas_call(crm_kernel, out_shape=(jax.ShapeDtypeStruct((COLS, 4 * LEV...  11.7 us
    unnamed x14, local copies, waits for them, and re-layouts  3.47 us

profile of v2, /device:TPU:6, one launch (start us, length us, event | category | flops | bytes accessed | tf_op | source)
XLA Modules:
  0.0 53.5 jit_solution(18252193252353933093)
XLA Ops:
  0.6 0.0 copy-start.4
  0.6 0.8 %copy.20.nbr_elem_ref = s32[16,4]{1,0:T(8,128)S(1)} copy(s32[16,4]{0,1:T(4,128)} %param.21) | data formatting | bytes 512 | tf_op args[5]
  1.4 0.0 copy-done.4
  1.4 0.1 copy.21.nbr_side_ref
  1.5 11.7 %shard_map.183 = (bf16[64,288]{1,0:T(8,128)(2,1)}, bf16[64,5568]{1,0:T(8,128)(2,1)}, f32[1,64]{1,0:T(1,128)}) custom-call(bf16[64,288]{1,0:T(8,128)(2,1)} %state_hbm.1, bf16[64,5568]{1,0:T(8,128)(2,1)} %fields_hbm.1, s32[64]{0:T(128)} %active_ref.1, f32[58]{0:T(128)} %density_hbm.1, bf16[128,256]{1,0:T(8,128)(2,1)} %constant.18.clone.dxm_hbm, ...), custom_call_target="tpu_custom_call" | custom-call | tf_op jit(solution)/shard_map/pallas_call | solution.py:352
  13.2 0.0 copy-start.1
  13.3 0.0 copy-start.2
  13.3 0.0 copy-start.3
  13.3 0.6 %copy-done.1 = s32[64]{0:T(128)S(1)} copy-done((s32[64]{0:T(128)S(1)}, s32[64]{0:T(128)}, u32[]{:S(2)}) %copy-start.1) | copy-done | bytes 280
  13.9 0.0 copy-done.2
  13.9 0.0 copy-done.3
  13.9 0.0 copy-start
  13.9 0.8 %copy-done = bf16[64,288]{1,0:T(8,128)(2,1)S(1)} copy-done((bf16[64,288]{1,0:T(8,128)(2,1)S(1)}, bf16[64,288]{1,0:T(8,128)(2,1)}, u32[]{:S(2)}) %copy-start) | copy-done | bytes 36888
  14.7 37.6 %shard_map.184 = (f32[16,4,288]{2,1,0:T(4,128)S(1)}, f32[1,24]{1,0:T(1,128)S(1)}) custom-call(bf16[64,288]{1,0:T(8,128)(2,1)S(1)} %copy-done, f32[1,64]{1,0:T(1,128)S(1)} %copy-done.3, s32[64]{0:T(128)S(1)} %copy-done.2, s32[64]{0:T(128)S(1)} %copy-done.1, s32[16,4]{1,0:T(8,128)S(1)} %copy.20.nbr_elem_ref, s32[16,4]{1,0:T(8,128)S(1)} %copy.21.nbr_side_ref), custom_call_target="tpu_custom_call" | custom-call | tf_op jit(solution)/shard_map/pallas_call | solution.py:503
  52.3 0.5 copy.24
  52.8 0.6 %copy.25 = f32[16,4,288]{2,1,0:T(4,128)} copy(f32[16,4,288]{2,1,0:T(4,128)S(1)} %get-tuple-element.21) | data formatting | bytes 147456
Async XLA Ops:
  0.6 0.8 %copy-start.4 = (s32[16,4]{0,1:T(4,128)S(1)}, s32[16,4]{0,1:T(4,128)}, u32[]{:S(2)}) copy-start(s32[16,4]{0,1:T(4,128)} %param.22) | copy-start | bytes 772
  13.2 0.7 %copy-start.1 = (s32[64]{0:T(128)S(1)}, s32[64]{0:T(128)}, u32[]{:S(2)}) copy-start(s32[64]{0:T(128)} %active_ref.1) | copy-start | bytes 772
  13.3 0.7 %copy-start.2 = (s32[64]{0:T(128)S(1)}, s32[64]{0:T(128)}, u32[]{:S(2)}) copy-start(s32[64]{0:T(128)} %span_map_ref.1) | copy-start | bytes 772
  13.3 0.7 %copy-start.3 = (f32[1,64]{1,0:T(1,128)S(1)}, f32[1,64]{1,0:T(1,128)}, u32[]{:S(2)}) copy-start(f32[1,64]{1,0:T(1,128)} %get-tuple-element.11.precip_ref) | copy-start | bytes 772
  13.9 0.8 %copy-start = (bf16[64,288]{1,0:T(8,128)(2,1)S(1)}, bf16[64,288]{1,0:T(8,128)(2,1)}, u32[]{:S(2)}) copy-start(bf16[64,288]{1,0:T(8,128)(2,1)} %get-tuple-element.18.tend_ref) | copy-start | bytes 110596

commit v3 on v2

--- a/solution.py
+++ b/solution.py
@@ -9,7 +9,6 @@
 from jax.experimental.pallas import tpu as pltpu
 from jax.sharding import PartitionSpec as P
 
-HIGH = lax.Precision.HIGHEST
 MESH = pl.DeviceIdType.MESH
 LEV, NZ, NX, COLS = 72, 58, 32, 64
 G, R, LANES = 4, 16, 128
@@ -106,22 +105,37 @@
 
 
 def crm_kernel(
-    state_hbm, fields_hbm, active_hbm, density_hbm,
+    shape,
+    state_hbm, fields_hbm, active_hbm, density_hbm, span_map_hbm, nbr_elem_hbm, nbr_side_hbm,
     dxm_hbm, forward_hbm, back_hbm, eigen_hbm, rise_hbm, spread_hbm, gather_hbm, tally_hbm, fall_hbm,
-    tend_hbm, fresh_hbm, precip_hbm,
-    state_ref, fields_ref, active_ref, density_ref, density_row_ref,
+    tend_hbm, fresh_hbm, rows_hbm, edge_hbm,
+    state_ref, fields_ref, active_ref, density_ref, span_map_ref, nbr_elem_ref, nbr_side_ref,
     dxm_ref, forward_ref, back_ref, eigen_ref, rise_ref, spread_ref, gather_ref, tally_ref, fall_ref,
-    tend_ref, fresh_ref, precip_ref,
+    tend_ref, fresh_ref, rows_ref, edge_ref,
     raw, dxm, prof_wide, prof_rows, inv, coup, u1, w1, left, sol, cells, pres, means, fresh,
-    in_sem, field_sem, out_sem, fresh_sem,
+    from_left, from_right, sent, got, from_lower, from_upper, flat,
+    in_sem, field_sem, out_sem, fresh_sem, send_sem, recv_sem, halo_send, halo_recv, relay_send, relay_recv,
 ):
+    regions, spans = shape
+    reach = spans // 4
+    region, span = lax.axis_index("region"), lax.axis_index("span")
+    me = region * spans + span
+    total = regions * spans
+    next_device, left_device = lax.rem(me + 1, total), lax.rem(me + total - 1, total)
+    next_device = (lax.div(next_device, spans), lax.rem(next_device, spans))
+    left_device = (lax.div(left_device, spans), lax.rem(left_device, spans))
+
+    def along(offset):
+        return (region, lax.rem(span + offset, spans))
+
     copies = {}
     pairs = dict(
         state=(state_hbm, state_ref), rise=(rise_hbm, rise_ref), active=(active_hbm, active_ref),
         spread=(spread_hbm, spread_ref), dxm=(dxm_hbm, dxm_ref), density=(density_hbm, density_ref),
         eigen=(eigen_hbm, eigen_ref), forward=(forward_hbm, forward_ref), back=(back_hbm, back_ref),
         gather=(gather_hbm, gather_ref), tally=(tally_hbm, tally_ref), fall=(fall_hbm, fall_ref),
-        density_row=(density_hbm, density_row_ref),
+        span_map=(span_map_hbm, span_map_ref), nbr_elem=(nbr_elem_hbm, nbr_elem_ref),
+        nbr_side=(nbr_side_hbm, nbr_side_ref),
     )
     for n, (name, (source, target)) in enumerate(pairs.items()):
         copies[name] = pltpu.make_async_copy(source, target, in_sem.at[n])
@@ -133,6 +147,17 @@
                 )
                 copies[k].start()
         copies[name].start()
+
+    barrier = pltpu.get_barrier_semaphore()
+
+    def greet(i, _):
+        for offset in (i, spans - i):
+            pl.semaphore_signal(barrier, inc=1, device_id=along(offset), device_id_type=MESH)
+        return _
+
+    lax.fori_loop(1, reach + 1, greet, 0)
+    for other in (left_device, next_device):
+        pl.semaphore_signal(barrier, inc=1, device_id=other, device_id_type=MESH)
 
     lane = lax.broadcasted_iota(jnp.int32, (R, LANES), 1)
     row = lax.broadcasted_iota(jnp.int32, (R, LANES), 0)
@@ -210,7 +235,7 @@
         return stores, (e_low, e_high, diag)
 
     def advect(z, carry):
-        (u_m, u), (w_m, w), (q_m, q), (rw_mm, rw_m) = carry
+        (u_m, u), (w_m, w), (q_m, q), (rw_mm, rw_m), rain = carry
         u_p, w_p, q_p = [raw[f, z + 2].astype(F32) for f in range(3)]
         rho = density_ref[z]
         half = 0.125 * w
@@ -233,7 +258,7 @@
             (left.at[:, :, : 2 * LANES], z + 1, jnp.concatenate(halves(rho * new_u), 1)),
             (left.at[:, :, 2 * LANES :], z, jnp.concatenate(halves(0.5 * (rw - rw_mm)), 1)),
         ]
-        return stores, ((u, u_p), (w, w_p), (q, q_p), (rw_m, rw))
+        return stores, ((u, u_p), (w, w_p), (q, q_p), (rw_m, rw), rain + rho * cond)
 
     def both_passes(t, carry):
         stores, last = factor(t, carry[0])
@@ -243,11 +268,58 @@
             ref[z] = value
         return last, levels
 
-    first = tuple((zero, raw[f, 1].astype(F32)) for f in range(3)) + ((zero, zero),)
+    first = tuple((zero, raw[f, 1].astype(F32)) for f in range(3)) + ((zero, zero), zero)
     last, levels = lax.fori_loop(0, NZ // 2, both_passes, ((zero, zero, zero), first))
     left[NZ, :, 2 * LANES :] = jnp.concatenate(halves(-0.5 * levels[3][0]), 1)
     mid = NZ // 2
     centre = 1.0 / (last[2] - 0.5 * (density_ref[mid - 1] + density_ref[mid]) * last[0])
+
+    copies["gather"].wait()
+    parts = dot(jnp.concatenate(halves(levels[4] * (2.0 / NZ)), 1), gather_ref[...])
+    precip = jnp.sum(jnp.where(own, parts, 0.0), 0, keepdims=True)[:, :COLS]
+    copies["span_map"].wait()
+    order = lax.broadcasted_iota(jnp.int32, (spans, COLS), 0) + span
+    target = jnp.where(order >= spans, order - spans, order)
+    hot = jnp.where((span_map_ref[...].reshape(1, COLS) == target) & (flags > 0.5), 1.0, 0.0)
+    upper = lax.broadcasted_iota(jnp.int32, (COLS, COLS), 0) < lax.broadcasted_iota(jnp.int32, (COLS, COLS), 1)
+    before = dot(hot.astype(BF16), jnp.where(upper, 1.0, 0.0).astype(BF16))
+    one = jnp.sum(jnp.where(before < 0.5, hot, 0.0) * precip, 1, keepdims=True)
+    two = jnp.sum(jnp.where(before > 0.5, hot, 0.0) * precip, 1, keepdims=True)
+    load = jnp.sum(hot, 1, keepdims=True)
+    place = lax.broadcasted_iota(jnp.int32, (spans, LANES), 1)
+    block = jnp.where(place == 0, one, jnp.where(place == 1, two, jnp.where(place == 2, load, 0.0)))
+    for i in range(spans):
+        sent[i] = block[i : i + 1]
+    got[span] = block[:1]
+
+    pl.semaphore_wait(barrier, 2 * reach + 2)
+    relays = [
+        pltpu.make_async_remote_copy(
+            src_ref=sent.at[pl.ds(first_row, count)], dst_ref=slot, send_sem=relay_send.at[n],
+            recv_sem=relay_recv.at[n], device_id=along(offset), device_id_type=MESH,
+        )
+        for n, (first_row, count, slot, offset) in enumerate(
+            (
+                (reach + 1, reach, from_lower, reach),
+                (2 * reach + 1, reach - 1, from_upper, spans - reach),
+            )
+        )
+    ]
+    for relay in relays:
+        relay.start()
+
+    def give(source, slot, offset):
+        pltpu.make_async_remote_copy(
+            src_ref=source, dst_ref=got.at[slot], send_sem=send_sem, recv_sem=recv_sem,
+            device_id=along(offset), device_id_type=MESH,
+        ).start()
+
+    def give_near(i, _):
+        for offset in (i, spans - i):
+            give(sent.at[offset], span, offset)
+        return _
+
+    lax.fori_loop(1, reach + 1, give_near, 0)
 
     def give_back(k):
         blocks = []
@@ -309,10 +381,9 @@
         fresh[pl.ds(NZ + z, 2)] = w_out
         cells[2, here] = change
 
-    copies["gather"].wait()
     for f in range(3):
-        total = dot(cells[f].reshape(ROWS, 2 * LANES), gather_ref[...])
-        means[f, :NZ] = total.reshape(NZ, R, LANES)
+        block = dot(cells[f].reshape(ROWS, 2 * LANES), gather_ref[...])
+        means[f, :NZ] = block.reshape(NZ, R, LANES)
     lane_high = lane < COLS
 
     @pl.loop(0, NZ // 2)
@@ -326,48 +397,122 @@
         left[here, :, : 3 * LANES] = jnp.concatenate(values, 2)
 
     copies["tally"].wait()
-    total = dot(tally_ref[...], left[:NZ, :, : 3 * LANES].reshape(ROWS, 3 * LANES))
-    copies["density_row"].wait()
-    weights = density_row_ref[...].reshape(1, NZ) * (2.0 / NZ)
-    precip = dot(weights, total[:NZ, :LANES], precision=HIGH)
-    precip_ref[...] = precip[:, :COLS] + precip[:, COLS:]
-    total = jnp.concatenate([total[:, LANES * f : LANES * f + LANES] for f in range(3)], 0)
-    t_high, t_low = halves(jnp.where(keep > 0.5, total, 0.0).T)
+    sums = dot(tally_ref[...], left[:NZ, :, : 3 * LANES].reshape(ROWS, 3 * LANES))
+    sums = jnp.concatenate([sums[:, LANES * f : LANES * f + LANES] for f in range(3)], 0)
+    t_high, t_low = halves(jnp.where(keep > 0.5, sums, 0.0).T)
     copies["fall"].wait()
     tend = dot(t_high, fall_ref[0]) + dot(t_low, fall_ref[0]) + dot(t_high, fall_ref[1])
     tend_ref[...] = (tend[:COLS] + tend[COLS:]).astype(BF16)
+    half = COLS // 2
+    halos = [
+        pltpu.make_async_remote_copy(
+            src_ref=tend_ref.at[part], dst_ref=slot, send_sem=halo_send.at[n], recv_sem=halo_recv.at[n],
+            device_id=other, device_id_type=MESH,
+        )
+        for n, (part, slot, other) in enumerate(
+            ((pl.ds(half, half), from_left, next_device), (pl.ds(0, half), from_right, left_device))
+        )
+    ]
+    for halo in halos:
+        halo.start()
     leaving.append(pltpu.make_async_copy(tend_ref, tend_hbm, out_sem.at[0]))
     leaving[-1].start()
-    leaving.append(pltpu.make_async_copy(precip_ref, precip_hbm, out_sem.at[1]))
+
+    for relay in relays:
+        relay.wait_recv()
+
+    def pass_up(i, _):
+        give(from_lower.at[i], lax.rem(span + spans - reach, spans), i + 1)
+        return _
+
+    def pass_down(i, _):
+        give(from_upper.at[i], lax.rem(span + reach, spans), spans - reach + 1 + i)
+        return _
+
+    lax.fori_loop(0, reach, pass_up, 0)
+    lax.fori_loop(0, reach - 1, pass_down, 0)
+
+    leaving += [give_back(k) for k in range(8)]
+
+    copies["nbr_elem"].wait()
+    copies["nbr_side"].wait()
+    elems = COLS // 4
+    cell = lax.broadcasted_iota(jnp.int32, (2 * COLS, elems), 0)
+    elem, corner = cell >> 2, cell & 3
+    c_low, c_high = corner & 1, corner >> 1
+    home = lax.broadcasted_iota(jnp.int32, (2 * COLS, elems), 1) + elems // 2
+    faces = (1 - c_high, c_low, c_high, 1 - c_low)
+    everyone = total * elems
+    picks = []
+    for side in range(4):
+        near = nbr_elem_ref[side : side + 1, :] - (me * elems - elems // 2)
+        near = jnp.where(near < 0, near + everyone, near)
+        near = jnp.where(near >= everyone, near - everyone, near)
+        theirs = nbr_side_ref[side : side + 1, :]
+        face = jnp.where(
+            theirs < 2, jnp.where(theirs == 0, faces[0], faces[1]), jnp.where(theirs == 2, faces[2], faces[3])
+        )
+        pick = jnp.where(near == elem, face, 0) + jnp.where(home == elem, faces[side], 0)
+        picks.append((0.5 * pick.astype(F32)).T.astype(BF16))
+
+    for halo in halos:
+        halo.wait()
+    table = jnp.concatenate([from_left[...], tend_ref[...], from_right[...]], 0)
+    for side in range(4):
+        edge_ref[:, side, :] = dot(picks[side], table)
+    leaving.append(pltpu.make_async_copy(edge_ref, edge_hbm, out_sem.at[1]))
     leaving[-1].start()
-    leaving += [give_back(k) for k in range(8)]
+    for relay in relays:
+        relay.wait_send()
+
+    lower = lax.broadcasted_iota(jnp.int32, (spans, spans), 0) > lax.broadcasted_iota(jnp.int32, (spans, spans), 1)
+    lower = jnp.where(lower, 1.0, 0.0).astype(BF16)
+    others = pl.ds(0, spans - 1)
+    pltpu.make_async_copy(got.at[others], got.at[others], recv_sem).wait()
+    for i in range(spans):
+        flat[i : i + 1] = got[i]
+    table = flat[...]
+    load = jnp.broadcast_to(table[:, 2:3], (spans, LANES))
+    start = dot(lower, load.astype(BF16))
+    slot = place.astype(F32)
+    rows = jnp.where((start == slot) & (load > 0.5), table[:, 0:1], 0.0)
+    rows += jnp.where((start + 1.0 == slot) & (load > 1.5), table[:, 1:2], 0.0)
+    rows_ref[...] = jnp.sum(rows, 0, keepdims=True)[:, : rows_ref.shape[1]]
+    leaving.append(pltpu.make_async_copy(rows_ref, rows_hbm, out_sem.at[2]))
+    leaving[-1].start()
+    pltpu.make_async_copy(sent.at[others], sent.at[others], send_sem).wait()
     for copy in leaving:
         copy.wait()
 
 
-def crm_call(column_state, crm_fields, active, density):
+def crm_call(shape, slots, column_state, crm_fields, active, density, span_map, nbr_elem, nbr_side):
     constants = [jnp.asarray(a) for a in tables()]
     hbm = pl.BlockSpec(memory_space=pltpu.HBM)
     levels = (NZ, R, LANES)
+    spans = shape[1]
     return pl.pallas_call(
-        crm_kernel,
+        functools.partial(crm_kernel, shape),
         out_shape=(
             jax.ShapeDtypeStruct((COLS, 4 * LEV), BF16),
             jax.ShapeDtypeStruct((COLS, 3 * NZ * NX), BF16),
-            jax.ShapeDtypeStruct((1, COLS), F32),
+            jax.ShapeDtypeStruct((1, slots), F32),
+            jax.ShapeDtypeStruct((COLS // 4, 4, 4 * LEV), F32),
         ),
-        in_specs=[hbm] * (4 + len(constants)),
-        out_specs=(hbm, hbm, hbm),
+        in_specs=[hbm] * (7 + len(constants)),
+        out_specs=(hbm,) * 4,
         scratch_shapes=[
             pltpu.VMEM((COLS, 4 * LEV), BF16),
             pltpu.VMEM((COLS, 3 * NZ * NX), BF16),
             pltpu.VMEM((COLS,), jnp.int32),
             pltpu.SMEM((NZ,), F32),
-            pltpu.VMEM((NZ,), F32),
+            pltpu.VMEM((COLS,), jnp.int32),
+            pltpu.VMEM((4, COLS // 4), jnp.int32),
+            pltpu.VMEM((4, COLS // 4), jnp.int32),
             *[pltpu.VMEM(a.shape, a.dtype) for a in constants],
             pltpu.VMEM((COLS, 4 * LEV), BF16),
             pltpu.VMEM((COLS, 3 * NZ * NX), BF16),
-            pltpu.VMEM((1, COLS), F32),
+            pltpu.VMEM((1, slots), F32),
+            pltpu.VMEM((COLS // 4, 4, 4 * LEV), F32),
             pltpu.VMEM((3, NZ + 2, R, LANES), BF16),
             pltpu.VMEM((3, NZ, R, 2 * LANES), F32),
             pltpu.VMEM((192, LANES), F32),
@@ -382,154 +527,69 @@
             pltpu.VMEM((NZ + 2, R, LANES), F32),
             pltpu.VMEM((3, 64, R, LANES), F32),
             pltpu.VMEM((3 * NZ, R, LANES), BF16),
-            pltpu.SemaphoreType.DMA((13,)),
-            pltpu.SemaphoreType.DMA((CHUNKS,)),
-            pltpu.SemaphoreType.DMA((2,)),
-            pltpu.SemaphoreType.DMA((CHUNKS,)),
-        ],
-        compiler_params=pltpu.CompilerParams(vmem_limit_bytes=63 * 2**20),
-    )(column_state, crm_fields, active, density, *constants)
-
-
-def exchange_kernel(
-    shape, tend_ref, precip_ref, span_map_ref, active_ref, nbr_elem_ref, nbr_side_ref,
-    edge_ref, rows_ref,
-    from_left, from_right, sent, got, flat, send_sem, recv_sem, halo_send, halo_recv,
-):
-    regions, spans = shape
-    region, span = lax.axis_index("region"), lax.axis_index("span")
-    me = region * spans + span
-    total = regions * spans
-    right, left = lax.rem(me + 1, total), lax.rem(me + total - 1, total)
-    right, left = (lax.div(right, spans), lax.rem(right, spans)), (lax.div(left, spans), lax.rem(left, spans))
-
-    barrier = pltpu.get_barrier_semaphore()
-
-    def greet(i, _):
-        pl.semaphore_signal(
-            barrier, inc=1, device_id=(region, lax.rem(span + i, spans)), device_id_type=MESH
-        )
-        return _
-
-    lax.fori_loop(1, spans, greet, 0)
-    for other in (left, right):
-        pl.semaphore_signal(barrier, inc=1, device_id=other, device_id_type=MESH)
-
-    target = lax.broadcasted_iota(jnp.int32, (spans, COLS), 0)
-    hot = jnp.where(
-        (span_map_ref[...].reshape(1, COLS) == target) & (active_ref[...].reshape(1, COLS) > 0), 1.0, 0.0
-    )
-    upper = lax.broadcasted_iota(jnp.int32, (COLS, COLS), 0) < lax.broadcasted_iota(jnp.int32, (COLS, COLS), 1)
-    before = dot(hot.astype(BF16), jnp.where(upper, 1.0, 0.0).astype(BF16))
-    precip = precip_ref[...]
-    one = jnp.sum(jnp.where(before < 0.5, hot, 0.0) * precip, 1, keepdims=True)
-    two = jnp.sum(jnp.where(before > 0.5, hot, 0.0) * precip, 1, keepdims=True)
-    load = jnp.sum(hot, 1, keepdims=True)
-    lane = lax.broadcasted_iota(jnp.int32, (spans, LANES), 1)
-    block = jnp.where(lane == 0, one, jnp.where(lane == 1, two, jnp.where(lane == 2, load, 0.0)))
-    for i in range(spans):
-        sent[i] = block[i : i + 1]
-    got[span] = sent[span]
-
-    pl.semaphore_wait(barrier, spans + 1)
-    half = COLS // 2
-    halos = [
-        pltpu.make_async_remote_copy(
-            src_ref=tend_ref.at[part], dst_ref=place, send_sem=halo_send.at[n], recv_sem=halo_recv.at[n],
-            device_id=other, device_id_type=MESH,
-        )
-        for n, (part, place, other) in enumerate(
-            ((pl.ds(half, half), from_left, right), (pl.ds(0, half), from_right, left))
-        )
-    ]
-    for halo in halos:
-        halo.start()
-
-    def give(i, _):
-        there = lax.rem(span + i, spans)
-        pltpu.make_async_remote_copy(
-            src_ref=sent.at[there], dst_ref=got.at[span], send_sem=send_sem, recv_sem=recv_sem,
-            device_id=(region, there), device_id_type=MESH,
-        ).start()
-        return _
-
-    lax.fori_loop(1, spans, give, 0)
-
-    cell = lax.broadcasted_iota(jnp.int32, (COLS // 4, 2 * COLS), 1)
-    elem, corner = cell >> 2, cell & 3
-    c_low, c_high = corner & 1, corner >> 1
-    home = lax.broadcasted_iota(jnp.int32, (COLS // 4, 2 * COLS), 0) + COLS // 8
-    faces = (1 - c_high, c_low, c_high, 1 - c_low)
-    everyone = total * (COLS // 4)
-    picks = []
-    for side in range(4):
-        near = nbr_elem_ref[:, side : side + 1] - (me * (COLS // 4) - COLS // 8)
-        near = jnp.where(near < 0, near + everyone, near)
-        near = jnp.where(near >= everyone, near - everyone, near)
-        theirs = nbr_side_ref[:, side : side + 1]
-        face = jnp.where(
-            theirs < 2, jnp.where(theirs == 0, faces[0], faces[1]), jnp.where(theirs == 2, faces[2], faces[3])
-        )
-        pick = jnp.where(near == elem, face, 0) + jnp.where(home == elem, faces[side], 0)
-        picks.append((0.5 * pick.astype(F32)).astype(BF16))
-
-    for halo in halos:
-        halo.wait()
-    own = tend_ref[...]
-    table = jnp.concatenate([from_left[...], own, from_right[...]], 0)
-    for side in range(4):
-        edge_ref[:, side, :] = dot(picks[side], table)
-
-    others = pl.ds(0, spans - 1)
-    pltpu.make_async_copy(got.at[others], got.at[others], recv_sem).wait()
-    for i in range(spans):
-        flat[i : i + 1] = got[i]
-    table = flat[...]
-    lower = lax.broadcasted_iota(jnp.int32, (spans, spans), 0) > lax.broadcasted_iota(jnp.int32, (spans, spans), 1)
-    load = table[:, 2:3]
-    start = dot(
-        jnp.where(lower, 1.0, 0.0).astype(BF16), jnp.broadcast_to(load, (spans, LANES)).astype(BF16)
-    )
-    place = lane.astype(F32)
-    rows = jnp.where((start == place) & (load > 0.5), table[:, 0:1], 0.0)
-    rows += jnp.where((start + 1.0 == place) & (load > 1.5), table[:, 1:2], 0.0)
-    rows_ref[...] = jnp.sum(rows, 0, keepdims=True)[:, : rows_ref.shape[1]]
-    pltpu.make_async_copy(sent.at[others], sent.at[others], send_sem).wait()
-
-
-def exchange_call(shape, slots, tendency, precip, span_map, active, nbr_elem, nbr_side):
-    spans = shape[1]
-    vmem = pl.BlockSpec(memory_space=pltpu.VMEM)
-    return pl.pallas_call(
-        functools.partial(exchange_kernel, shape),
-        out_shape=(
-            jax.ShapeDtypeStruct((COLS // 4, 4, 4 * LEV), F32),
-            jax.ShapeDtypeStruct((1, slots), F32),
-        ),
-        in_specs=[vmem] * 6,
-        out_specs=(vmem, vmem),
-        scratch_shapes=[
             pltpu.VMEM((COLS // 2, 4 * LEV), BF16),
             pltpu.VMEM((COLS // 2, 4 * LEV), BF16),
             pltpu.VMEM((spans, 1, LANES), F32),
             pltpu.VMEM((spans, 1, LANES), F32),
+            pltpu.VMEM((spans // 4, 1, LANES), F32),
+            pltpu.VMEM((spans // 4 - 1, 1, LANES), F32),
             pltpu.VMEM((spans, LANES), F32),
+            pltpu.SemaphoreType.DMA((15,)),
+            pltpu.SemaphoreType.DMA((CHUNKS,)),
+            pltpu.SemaphoreType.DMA((3,)),
+            pltpu.SemaphoreType.DMA((CHUNKS,)),
             pltpu.SemaphoreType.DMA,
             pltpu.SemaphoreType.DMA,
             pltpu.SemaphoreType.DMA((2,)),
             pltpu.SemaphoreType.DMA((2,)),
+            pltpu.SemaphoreType.DMA((2,)),
+            pltpu.SemaphoreType.DMA((2,)),
         ],
         compiler_params=pltpu.CompilerParams(
-            collective_id=0, has_side_effects=True, vmem_limit_bytes=16 * 2**20
+            collective_id=0, has_side_effects=True, vmem_limit_bytes=63 * 2**20
         ),
-    )(tendency, precip, span_map, active, nbr_elem, nbr_side)
+    )(column_state, crm_fields, active, density, span_map, nbr_elem.T, nbr_side.T, *constants)
+
+
+def hand_over_kernel(*refs):
+    count = (len(refs) - 2) // 3
+    came, went = refs[-2:]
+    pieces = []
+    for source, target, stage in zip(refs[:count], refs[count:], refs[2 * count :]):
+        rows = source.shape[0]
+        step = rows // 4 if rows == COLS and source.shape[1] > 4 * LEV else rows
+        for top in range(0, rows, step):
+            cut = pl.ds(top, step)
+            pieces.append((source.at[cut], stage.at[cut], target.at[cut]))
+    inward = [pltpu.make_async_copy(a, b, came.at[n]) for n, (a, b, _) in enumerate(pieces)]
+    outward = [pltpu.make_async_copy(b, c, went.at[n]) for n, (_, b, c) in enumerate(pieces)]
+    for copy in inward:
+        copy.start()
+    for first, second in zip(inward, outward):
+        first.wait()
+        second.start()
+    for copy in outward:
+        copy.wait()
+
+
+def hand_over(*arrays):
+    hbm = pl.BlockSpec(memory_space=pltpu.HBM)
+    return pl.pallas_call(
+        hand_over_kernel,
+        out_shape=tuple(jax.ShapeDtypeStruct(a.shape, a.dtype) for a in arrays),
+        in_specs=[hbm] * len(arrays),
+        out_specs=(hbm,) * len(arrays),
+        scratch_shapes=[pltpu.VMEM(a.shape, a.dtype) for a in arrays]
+        + [pltpu.SemaphoreType.DMA((len(arrays) + 3,))] * 2,
+        compiler_params=pltpu.CompilerParams(vmem_limit_bytes=63 * 2**20),
+    )(*arrays)
 
 
 def body(shape, column_state, crm_fields, span_map, active, density, nbr_elem, nbr_side):
-    tendency, fresh, precip = crm_call(column_state, crm_fields, active, density)
-    edge_sums, rows = exchange_call(
-        shape, COLS * 3 // 8, tendency, precip, span_map, active, nbr_elem, nbr_side
+    results = crm_call(
+        shape, COLS * 3 // 8, column_state, crm_fields, active, density, span_map, nbr_elem, nbr_side
     )
+    tendency, fresh, rows, edge_sums = hand_over(*results)
     return (tendency, fresh, rows[0], edge_sums)
 
 

time: 53.7 us -> 41.8 us (0.78)
  Pallas kernels: 49.3 us -> 41 us
  local copies, waits for them, and re-layouts: 3.47 us -> 0 us
    pallas_call x2, Pallas kernels: 49.3 us -> 41 us  [the longest x1 39 us: crm_call(): pl.pallas_call(functools.partial(crm_kernel, shape), out_shape=(jax.Shape...]
    unnamed x14 -> x0, local copies, waits for them, and re-layouts: 3.47 us -> none
where the time goes in v3:
time: 41.8 us; the launch traced here: 41.6 us
  Pallas kernels  41 us (98%)
  between operations  0.64 us (2%)
    pallas_call x1, Pallas kernels, crm_call(): pl.pallas_call(functools.partial(crm_kernel, shape), out_shape=(jax.Shape...  39 us
    pallas_call x1, Pallas kernels, hand_over(): pl.pallas_call(hand_over_kernel, out_shape=tuple((jax.ShapeDtypeStruct(a....  2.04 us

profile of v3, /device:TPU:6, one launch (start us, length us, event | category | flops | bytes accessed | tf_op | source)
XLA Modules:
  0.0 41.6 jit_solution(10028513433622526218)
XLA Ops:
  0.6 39.0 %shard_map.183 = (bf16[64,288]{1,0:T(8,128)(2,1)}, bf16[64,5568]{1,0:T(8,128)(2,1)}, f32[1,24]{1,0:T(1,128)}, f32[16,4,288]{2,1,0:T(4,128)}) custom-call(bf16[64,288]{1,0:T(8,128)(2,1)} %state_hbm.1, bf16[64,5568]{1,0:T(8,128)(2,1)} %fields_hbm.1, s32[64]{0:T(128)} %active_hbm.1, f32[58]{0:T(128)} %density_hbm.1, s32[64]{0:T(128)} %span_map_hbm.1, ...), custom_call_target="tpu_custom_call" | custom-call | tf_op jit(solution)/shard_map/pallas_call | solution.py:493
  39.6 2.0 %shard_map.184 = (bf16[64,288]{1,0:T(8,128)(2,1)}, bf16[64,5568]{1,0:T(8,128)(2,1)}, f32[1,24]{1,0:T(1,128)}, f32[16,4,288]{2,1,0:T(4,128)}) custom-call(bf16[64,288]{1,0:T(8,128)(2,1)} %get-tuple-element.12.refs_0_, bf16[64,5568]{1,0:T(8,128)(2,1)} %get-tuple-element.13.refs_1_, f32[1,24]{1,0:T(1,128)} %get-tuple-element.14.refs_2_, ...), custom_call_target="tpu_custom_call" | custom-call | tf_op jit(solution)/shard_map/pallas_call | solution.py:577

commit v4 on v3

--- a/solution.py
+++ b/solution.py
@@ -108,13 +108,12 @@
     shape,
     state_hbm, fields_hbm, active_hbm, density_hbm, span_map_hbm, nbr_elem_hbm, nbr_side_hbm,
     dxm_hbm, forward_hbm, back_hbm, eigen_hbm, rise_hbm, spread_hbm, gather_hbm, tally_hbm, fall_hbm,
-    tend_hbm, fresh_hbm, rows_hbm, edge_hbm,
+    tend_ref, fresh_ref, got, edge_ref,
     state_ref, fields_ref, active_ref, density_ref, span_map_ref, nbr_elem_ref, nbr_side_ref,
     dxm_ref, forward_ref, back_ref, eigen_ref, rise_ref, spread_ref, gather_ref, tally_ref, fall_ref,
-    tend_ref, fresh_ref, rows_ref, edge_ref,
     raw, dxm, prof_wide, prof_rows, inv, coup, u1, w1, left, sol, cells, pres, means, fresh,
-    from_left, from_right, sent, got, from_lower, from_upper, flat,
-    in_sem, field_sem, out_sem, fresh_sem, send_sem, recv_sem, halo_send, halo_recv, relay_send, relay_recv,
+    from_left, from_right, sent, from_lower, from_upper,
+    in_sem, field_sem, out_sem, send_sem, recv_sem, halo_send, halo_recv, relay_send, relay_recv,
 ):
     regions, spans = shape
     reach = spans // 4
@@ -127,6 +126,17 @@
 
     def along(offset):
         return (region, lax.rem(span + offset, spans))
+
+    barrier = pltpu.get_barrier_semaphore()
+
+    def greet(i, _):
+        for offset in (reach - i, spans - reach + i):
+            pl.semaphore_signal(barrier, inc=1, device_id=along(offset), device_id_type=MESH)
+        return _
+
+    lax.fori_loop(0, reach, greet, 0)
+    for other in (left_device, next_device):
+        pl.semaphore_signal(barrier, inc=1, device_id=other, device_id_type=MESH)
 
     copies = {}
     pairs = dict(
@@ -147,17 +157,6 @@
                 )
                 copies[k].start()
         copies[name].start()
-
-    barrier = pltpu.get_barrier_semaphore()
-
-    def greet(i, _):
-        for offset in (i, spans - i):
-            pl.semaphore_signal(barrier, inc=1, device_id=along(offset), device_id_type=MESH)
-        return _
-
-    lax.fori_loop(1, reach + 1, greet, 0)
-    for other in (left_device, next_device):
-        pl.semaphore_signal(barrier, inc=1, device_id=other, device_id_type=MESH)
 
     lane = lax.broadcasted_iota(jnp.int32, (R, LANES), 1)
     row = lax.broadcasted_iota(jnp.int32, (R, LANES), 0)
@@ -287,10 +286,11 @@
     two = jnp.sum(jnp.where(before > 0.5, hot, 0.0) * precip, 1, keepdims=True)
     load = jnp.sum(hot, 1, keepdims=True)
     place = lax.broadcasted_iota(jnp.int32, (spans, LANES), 1)
-    block = jnp.where(place == 0, one, jnp.where(place == 1, two, jnp.where(place == 2, load, 0.0)))
+    block = jnp.where(place < 32, load, jnp.where(place < 64, one, two))
     for i in range(spans):
         sent[i] = block[i : i + 1]
-    got[span] = block[:1]
+    mine = pltpu.make_async_copy(sent.at[0], got.at[span], out_sem)
+    mine.start()
 
     pl.semaphore_wait(barrier, 2 * reach + 2)
     relays = [
@@ -315,11 +315,11 @@
         ).start()
 
     def give_near(i, _):
-        for offset in (i, spans - i):
+        for offset in (reach - i, spans - reach + i):
             give(sent.at[offset], span, offset)
         return _
 
-    lax.fori_loop(1, reach + 1, give_near, 0)
+    lax.fori_loop(0, reach, give_near, 0)
 
     def give_back(k):
         blocks = []
@@ -334,12 +334,9 @@
                     fresh_ref[R * g : R * g + R, LANES * j : LANES * j + LANES] = part
                 else:
                     fresh_ref[R * g : R * g + R, LANES * j :] = part[:, :64]
-        cut = slice(WIDE * k, min(WIDE * k + WIDE, NZ * NX * 3))
-        copy = pltpu.make_async_copy(fresh_ref.at[:, cut], fresh_hbm.at[:, cut], fresh_sem.at[k])
-        copy.start()
-        return copy
-
-    leaving = [give_back(k) for k in range(8, CHUNKS)]
+
+    for k in range(8, CHUNKS):
+        give_back(k)
 
     copies["forward"].wait()
     right = dot(left[1:].reshape(ROWS, 4 * LANES), forward_ref[...])
@@ -415,24 +412,23 @@
     ]
     for halo in halos:
         halo.start()
-    leaving.append(pltpu.make_async_copy(tend_ref, tend_hbm, out_sem.at[0]))
-    leaving[-1].start()
 
     for relay in relays:
         relay.wait_recv()
 
-    def pass_up(i, _):
+    def pass_up(i):
         give(from_lower.at[i], lax.rem(span + spans - reach, spans), i + 1)
-        return _
-
-    def pass_down(i, _):
+
+    def pass_on(i, _):
+        pass_up(reach - 1 - i)
         give(from_upper.at[i], lax.rem(span + reach, spans), spans - reach + 1 + i)
         return _
 
-    lax.fori_loop(0, reach, pass_up, 0)
-    lax.fori_loop(0, reach - 1, pass_down, 0)
-
-    leaving += [give_back(k) for k in range(8)]
+    lax.fori_loop(0, reach - 1, pass_on, 0)
+    pass_up(0)
+
+    for k in range(8):
+        give_back(k)
 
     copies["nbr_elem"].wait()
     copies["nbr_side"].wait()
@@ -460,33 +456,18 @@
     table = jnp.concatenate([from_left[...], tend_ref[...], from_right[...]], 0)
     for side in range(4):
         edge_ref[:, side, :] = dot(picks[side], table)
-    leaving.append(pltpu.make_async_copy(edge_ref, edge_hbm, out_sem.at[1]))
-    leaving[-1].start()
     for relay in relays:
         relay.wait_send()
 
-    lower = lax.broadcasted_iota(jnp.int32, (spans, spans), 0) > lax.broadcasted_iota(jnp.int32, (spans, spans), 1)
-    lower = jnp.where(lower, 1.0, 0.0).astype(BF16)
     others = pl.ds(0, spans - 1)
+    mine.wait()
     pltpu.make_async_copy(got.at[others], got.at[others], recv_sem).wait()
-    for i in range(spans):
-        flat[i : i + 1] = got[i]
-    table = flat[...]
-    load = jnp.broadcast_to(table[:, 2:3], (spans, LANES))
-    start = dot(lower, load.astype(BF16))
-    slot = place.astype(F32)
-    rows = jnp.where((start == slot) & (load > 0.5), table[:, 0:1], 0.0)
-    rows += jnp.where((start + 1.0 == slot) & (load > 1.5), table[:, 1:2], 0.0)
-    rows_ref[...] = jnp.sum(rows, 0, keepdims=True)[:, : rows_ref.shape[1]]
-    leaving.append(pltpu.make_async_copy(rows_ref, rows_hbm, out_sem.at[2]))
-    leaving[-1].start()
     pltpu.make_async_copy(sent.at[others], sent.at[others], send_sem).wait()
-    for copy in leaving:
-        copy.wait()
-
-
-def crm_call(shape, slots, column_state, crm_fields, active, density, span_map, nbr_elem, nbr_side):
+
+
+def crm_call(shape, column_state, crm_fields, active, density, span_map, nbr_elem, nbr_side):
     constants = [jnp.asarray(a) for a in tables()]
+    operands = (column_state, crm_fields, active, density, span_map, nbr_elem.T, nbr_side.T, *constants)
     hbm = pl.BlockSpec(memory_space=pltpu.HBM)
     levels = (NZ, R, LANES)
     spans = shape[1]
@@ -495,11 +476,11 @@
         out_shape=(
             jax.ShapeDtypeStruct((COLS, 4 * LEV), BF16),
             jax.ShapeDtypeStruct((COLS, 3 * NZ * NX), BF16),
-            jax.ShapeDtypeStruct((1, slots), F32),
+            jax.ShapeDtypeStruct((spans, 1, LANES), F32),
             jax.ShapeDtypeStruct((COLS // 4, 4, 4 * LEV), F32),
         ),
         in_specs=[hbm] * (7 + len(constants)),
-        out_specs=(hbm,) * 4,
+        out_specs=(pl.BlockSpec(memory_space=pltpu.VMEM),) * 4,
         scratch_shapes=[
             pltpu.VMEM((COLS, 4 * LEV), BF16),
             pltpu.VMEM((COLS, 3 * NZ * NX), BF16),
@@ -509,10 +490,6 @@
             pltpu.VMEM((4, COLS // 4), jnp.int32),
             pltpu.VMEM((4, COLS // 4), jnp.int32),
             *[pltpu.VMEM(a.shape, a.dtype) for a in constants],
-            pltpu.VMEM((COLS, 4 * LEV), BF16),
-            pltpu.VMEM((COLS, 3 * NZ * NX), BF16),
-            pltpu.VMEM((1, slots), F32),
-            pltpu.VMEM((COLS // 4, 4, 4 * LEV), F32),
             pltpu.VMEM((3, NZ + 2, R, LANES), BF16),
             pltpu.VMEM((3, NZ, R, 2 * LANES), F32),
             pltpu.VMEM((192, LANES), F32),
@@ -530,14 +507,11 @@
             pltpu.VMEM((COLS // 2, 4 * LEV), BF16),
             pltpu.VMEM((COLS // 2, 4 * LEV), BF16),
             pltpu.VMEM((spans, 1, LANES), F32),
-            pltpu.VMEM((spans, 1, LANES), F32),
             pltpu.VMEM((spans // 4, 1, LANES), F32),
             pltpu.VMEM((spans // 4 - 1, 1, LANES), F32),
-            pltpu.VMEM((spans, LANES), F32),
             pltpu.SemaphoreType.DMA((15,)),
             pltpu.SemaphoreType.DMA((CHUNKS,)),
-            pltpu.SemaphoreType.DMA((3,)),
-            pltpu.SemaphoreType.DMA((CHUNKS,)),
+            pltpu.SemaphoreType.DMA,
             pltpu.SemaphoreType.DMA,
             pltpu.SemaphoreType.DMA,
             pltpu.SemaphoreType.DMA((2,)),
@@ -546,50 +520,61 @@
             pltpu.SemaphoreType.DMA((2,)),
         ],
         compiler_params=pltpu.CompilerParams(
-            collective_id=0, has_side_effects=True, vmem_limit_bytes=63 * 2**20
+            collective_id=0, has_side_effects=True, vmem_limit_bytes=40 * 2**20
         ),
-    )(column_state, crm_fields, active, density, span_map, nbr_elem.T, nbr_side.T, *constants)
-
-
-def hand_over_kernel(*refs):
-    count = (len(refs) - 2) // 3
-    came, went = refs[-2:]
-    pieces = []
-    for source, target, stage in zip(refs[:count], refs[count:], refs[2 * count :]):
-        rows = source.shape[0]
-        step = rows // 4 if rows == COLS and source.shape[1] > 4 * LEV else rows
-        for top in range(0, rows, step):
-            cut = pl.ds(top, step)
-            pieces.append((source.at[cut], stage.at[cut], target.at[cut]))
-    inward = [pltpu.make_async_copy(a, b, came.at[n]) for n, (a, b, _) in enumerate(pieces)]
-    outward = [pltpu.make_async_copy(b, c, went.at[n]) for n, (_, b, c) in enumerate(pieces)]
-    for copy in inward:
+    )(*[pltpu.with_memory_space_constraint(a, pltpu.HBM) for a in operands])
+
+
+def finish_kernel(tend, fresh, got, edge, tend_out, fresh_out, rows_out, edge_out, flat, rows_ref, went):
+    pieces = [(tend, tend_out), (edge, edge_out)]
+    for top in range(0, COLS, R):
+        cut = pl.ds(top, R)
+        pieces.append((fresh.at[cut], fresh_out.at[cut]))
+    outward = [pltpu.make_async_copy(a, b, went.at[n]) for n, (a, b) in enumerate(pieces)]
+    for copy in outward:
         copy.start()
-    for first, second in zip(inward, outward):
-        first.wait()
-        second.start()
+
+    spans = got.shape[0]
+    for i in range(spans):
+        flat[i : i + 1] = got[i]
+    table = flat[...]
+    lower = lax.broadcasted_iota(jnp.int32, (spans, spans), 0) > lax.broadcasted_iota(jnp.int32, (spans, spans), 1)
+    start = dot(jnp.where(lower, 1.0, 0.0).astype(BF16), table.astype(BF16))
+    one, two = pltpu.roll(table, LANES - 32, 1), pltpu.roll(table, LANES - 64, 1)
+    slot = lax.broadcasted_iota(jnp.int32, (spans, LANES), 1).astype(F32)
+    rows = jnp.where((start == slot) & (table > 0.5), one, 0.0)
+    rows += jnp.where((start + 1.0 == slot) & (table > 1.5), two, 0.0)
+    rows_ref[...] = jnp.sum(rows, 0, keepdims=True)[:, : rows_ref.shape[1]]
+    last = pltpu.make_async_copy(rows_ref, rows_out, went.at[len(pieces)])
+    last.start()
     for copy in outward:
         copy.wait()
-
-
-def hand_over(*arrays):
-    hbm = pl.BlockSpec(memory_space=pltpu.HBM)
+    last.wait()
+
+
+def finish(slots, tendency, fresh, got, edges):
+    hbm, vmem = pl.BlockSpec(memory_space=pltpu.HBM), pl.BlockSpec(memory_space=pltpu.VMEM)
+    shapes = [jax.ShapeDtypeStruct(a.shape, a.dtype) for a in (tendency, fresh, got, edges)]
+    shapes[2] = jax.ShapeDtypeStruct((1, slots), F32)
     return pl.pallas_call(
-        hand_over_kernel,
-        out_shape=tuple(jax.ShapeDtypeStruct(a.shape, a.dtype) for a in arrays),
-        in_specs=[hbm] * len(arrays),
-        out_specs=(hbm,) * len(arrays),
-        scratch_shapes=[pltpu.VMEM(a.shape, a.dtype) for a in arrays]
-        + [pltpu.SemaphoreType.DMA((len(arrays) + 3,))] * 2,
-        compiler_params=pltpu.CompilerParams(vmem_limit_bytes=63 * 2**20),
-    )(*arrays)
+        finish_kernel,
+        out_shape=tuple(shapes),
+        in_specs=[vmem] * 4,
+        out_specs=(hbm,) * 4,
+        scratch_shapes=[
+            pltpu.VMEM((got.shape[0], LANES), F32),
+            pltpu.VMEM((1, slots), F32),
+            pltpu.SemaphoreType.DMA((7,)),
+        ],
+        compiler_params=pltpu.CompilerParams(vmem_limit_bytes=16 * 2**20),
+    )(tendency, fresh, got, edges)
 
 
 def body(shape, column_state, crm_fields, span_map, active, density, nbr_elem, nbr_side):
     results = crm_call(
-        shape, COLS * 3 // 8, column_state, crm_fields, active, density, span_map, nbr_elem, nbr_side
+        shape, column_state, crm_fields, active, density, span_map, nbr_elem, nbr_side
     )
-    tendency, fresh, rows, edge_sums = hand_over(*results)
+    tendency, fresh, rows, edge_sums = finish(COLS * 3 // 8, *results)
     return (tendency, fresh, rows[0], edge_sums)
 
 

time: 41.8 us -> 40 us (0.957)
  Pallas kernels: 41 us -> 39.2 us
    pallas_call x1, Pallas kernels: 2.04 us -> 0.96 us  [finish(): pl.pallas_call(finish_kernel, out_shape=tuple(shapes), in_specs=[vmem] *...]
    pallas_call x1, Pallas kernels: 39 us -> 38.2 us  [crm_call(): pl.pallas_call(functools.partial(crm_kernel, shape), out_shape=(jax.Shape...]
where the time goes in v4:
time: 40 us; the launch traced here: 39.8 us
  Pallas kernels  39.2 us (98%)
  between operations  0.64 us (2%)
    pallas_call x1, Pallas kernels, crm_call(): pl.pallas_call(functools.partial(crm_kernel, shape), out_shape=(jax.Shape...  38.2 us
    pallas_call x1, Pallas kernels, finish(): pl.pallas_call(finish_kernel, out_shape=tuple(shapes), in_specs=[vmem] *...  0.96 us

profile of v4, /device:TPU:6, one launch (start us, length us, event | category | flops | bytes accessed | tf_op | source)
XLA Modules:
  0.0 39.8 jit_solution(10053103616349143363)
XLA Ops:
  0.6 38.2 %shard_map.183 = (bf16[64,288]{1,0:T(8,128)(2,1)S(1)}, bf16[64,5568]{1,0:T(8,128)(2,1)S(1)}, f32[32,1,128]{2,1,0:T(1,128)S(1)}, f32[16,4,288]{2,1,0:T(4,128)S(1)}) custom-call(bf16[64,288]{1,0:T(8,128)(2,1)} %state_hbm.1, bf16[64,5568]{1,0:T(8,128)(2,1)} %fields_hbm.1, s32[64]{0:T(128)} %active_hbm.1, f32[58]{0:T(128)} %density_hbm.1, s32[64]{0:T(128)} %span_map_hbm.1, ...), custom_call_target="tpu_custom_call" | custom-call | tf_op jit(solution)/shard_map/pallas_call | solution.py:474
  38.9 1.0 %shard_map.184 = (bf16[64,288]{1,0:T(8,128)(2,1)}, bf16[64,5568]{1,0:T(8,128)(2,1)}, f32[1,24]{1,0:T(1,128)}, f32[16,4,288]{2,1,0:T(4,128)}) custom-call(bf16[64,288]{1,0:T(8,128)(2,1)S(1)} %get-tuple-element.12.tend, bf16[64,5568]{1,0:T(8,128)(2,1)S(1)} %get-tuple-element.13.fresh, f32[32,1,128]{2,1,0:T(1,128)S(1)} %get-tuple-element.14.got, ...), custom_call_target="tpu_custom_call" | custom-call | tf_op jit(solution)/shard_map/pallas_call | solution.py:559

commit v5 on v4

--- a/solution.py
+++ b/solution.py
@@ -113,7 +113,7 @@
     dxm_ref, forward_ref, back_ref, eigen_ref, rise_ref, spread_ref, gather_ref, tally_ref, fall_ref,
     raw, dxm, prof_wide, prof_rows, inv, coup, u1, w1, left, sol, cells, pres, means, fresh,
     from_left, from_right, sent, from_lower, from_upper,
-    in_sem, field_sem, out_sem, send_sem, recv_sem, halo_send, halo_recv, relay_send, relay_recv,
+    in_sem, field_sem, out_sem, send_sem, recv_sem, pass_sem, halo_send, halo_recv, relay_send, relay_recv,
 ):
     regions, spans = shape
     reach = spans // 4
@@ -124,8 +124,11 @@
     next_device = (lax.div(next_device, spans), lax.rem(next_device, spans))
     left_device = (lax.div(left_device, spans), lax.rem(left_device, spans))
 
-    def along(offset):
-        return (region, lax.rem(span + offset, spans))
+    parity = lax.rem(region, 2)
+    lead = region + 1 - parity
+
+    def along(offset, where=region):
+        return (where, lax.rem(span + offset, spans))
 
     barrier = pltpu.get_barrier_semaphore()
 
@@ -133,6 +136,22 @@
         for offset in (reach - i, spans - reach + i):
             pl.semaphore_signal(barrier, inc=1, device_id=along(offset), device_id_type=MESH)
         return _
+
+    def greet_lead(i, _):
+        for offset in (reach - i, spans - reach + i):
+            pl.semaphore_signal(barrier, inc=1, device_id=along(offset, lead), device_id_type=MESH)
+        return _
+
+    @pl.when(parity == 0)
+    def _():
+        lax.fori_loop(0, reach, greet_lead, 0)
+
+    @pl.when(parity == 1)
+    def _():
+        for offset in (reach, spans - reach):
+            pl.semaphore_signal(
+                barrier, inc=1, device_id=along(offset, region - 1), device_id_type=MESH
+            )
 
     lax.fori_loop(0, reach, greet, 0)
     for other in (left_device, next_device):
@@ -292,11 +311,11 @@
     mine = pltpu.make_async_copy(sent.at[0], got.at[span], out_sem)
     mine.start()
 
-    pl.semaphore_wait(barrier, 2 * reach + 2)
+    pl.semaphore_wait(barrier, jnp.where(parity == 0, 2 * reach + 4, 4 * reach + 2))
     relays = [
         pltpu.make_async_remote_copy(
-            src_ref=sent.at[pl.ds(first_row, count)], dst_ref=slot, send_sem=relay_send.at[n],
-            recv_sem=relay_recv.at[n], device_id=along(offset), device_id_type=MESH,
+            src_ref=sent.at[pl.ds(first_row, count)], dst_ref=slot.at[parity], send_sem=relay_send.at[n],
+            recv_sem=relay_recv.at[n, parity], device_id=along(offset, lead), device_id_type=MESH,
         )
         for n, (first_row, count, slot, offset) in enumerate(
             (
@@ -308,10 +327,10 @@
     for relay in relays:
         relay.start()
 
-    def give(source, slot, offset):
+    def give(source, slot, offset, sem=send_sem, where=region):
         pltpu.make_async_remote_copy(
-            src_ref=source, dst_ref=got.at[slot], send_sem=send_sem, recv_sem=recv_sem,
-            device_id=along(offset), device_id_type=MESH,
+            src_ref=source, dst_ref=got.at[slot], send_sem=sem, recv_sem=recv_sem,
+            device_id=along(offset, where), device_id_type=MESH,
         ).start()
 
     def give_near(i, _):
@@ -413,19 +432,27 @@
     for halo in halos:
         halo.start()
 
-    for relay in relays:
-        relay.wait_recv()
-
-    def pass_up(i):
-        give(from_lower.at[i], lax.rem(span + spans - reach, spans), i + 1)
-
-    def pass_on(i, _):
-        pass_up(reach - 1 - i)
-        give(from_upper.at[i], lax.rem(span + reach, spans), spans - reach + 1 + i)
-        return _
-
-    lax.fori_loop(0, reach - 1, pass_on, 0)
-    pass_up(0)
+    passed = pl.ds(0, 4 * reach - 2)
+
+    @pl.when(parity == 1)
+    def _():
+        for n, slot in enumerate((from_lower, from_upper)):
+            for p in range(2):
+                pltpu.make_async_copy(slot.at[p], slot.at[p], relay_recv.at[n, p]).wait()
+        below, above = lax.rem(span + spans - reach, spans), lax.rem(span + reach, spans)
+
+        def pass_up(i):
+            for p in range(2):
+                give(from_lower.at[p, i], below, i + 1, pass_sem, region - 1 + p)
+
+        def pass_on(i, _):
+            pass_up(reach - 1 - i)
+            for p in range(2):
+                give(from_upper.at[p, i], above, spans - reach + 1 + i, pass_sem, region - 1 + p)
+            return _
+
+        lax.fori_loop(0, reach - 1, pass_on, 0)
+        pass_up(0)
 
     for k in range(8):
         give_back(k)
@@ -462,7 +489,12 @@
     others = pl.ds(0, spans - 1)
     mine.wait()
     pltpu.make_async_copy(got.at[others], got.at[others], recv_sem).wait()
-    pltpu.make_async_copy(sent.at[others], sent.at[others], send_sem).wait()
+    near = pl.ds(0, 2 * reach)
+    pltpu.make_async_copy(sent.at[near], sent.at[near], send_sem).wait()
+
+    @pl.when(parity == 1)
+    def _():
+        pltpu.make_async_copy(sent.at[passed], sent.at[passed], pass_sem).wait()
 
 
 def crm_call(shape, column_state, crm_fields, active, density, span_map, nbr_elem, nbr_side):
@@ -507,17 +539,18 @@
             pltpu.VMEM((COLS // 2, 4 * LEV), BF16),
             pltpu.VMEM((COLS // 2, 4 * LEV), BF16),
             pltpu.VMEM((spans, 1, LANES), F32),
-            pltpu.VMEM((spans // 4, 1, LANES), F32),
-            pltpu.VMEM((spans // 4 - 1, 1, LANES), F32),
+            pltpu.VMEM((2, spans // 4, 1, LANES), F32),
+            pltpu.VMEM((2, spans // 4 - 1, 1, LANES), F32),
             pltpu.SemaphoreType.DMA((15,)),
             pltpu.SemaphoreType.DMA((CHUNKS,)),
+            pltpu.SemaphoreType.DMA,
             pltpu.SemaphoreType.DMA,
             pltpu.SemaphoreType.DMA,
             pltpu.SemaphoreType.DMA,
             pltpu.SemaphoreType.DMA((2,)),
             pltpu.SemaphoreType.DMA((2,)),
             pltpu.SemaphoreType.DMA((2,)),
-            pltpu.SemaphoreType.DMA((2,)),
+            pltpu.SemaphoreType.DMA((2, 2)),
         ],
         compiler_params=pltpu.CompilerParams(
             collective_id=0, has_side_effects=True, vmem_limit_bytes=40 * 2**20

time: 40 us -> 40.3 us (level)
  the two profiles are of different devices: /device:TPU:6 before, /device:TPU:1 now
where the time goes in v5:
time: 40.3 us; the launch traced here: 40.1 us
  Pallas kernels  39.5 us (98%)
  between operations  0.64 us (2%)
    pallas_call x1, Pallas kernels, crm_call(): pl.pallas_call(functools.partial(crm_kernel, shape), out_shape=(jax.Shape...  38.5 us
    pallas_call x1, Pallas kernels, finish(): pl.pallas_call(finish_kernel, out_shape=tuple(shapes), in_specs=[vmem] *...  0.96 us

profile of v5, /device:TPU:1, one launch (start us, length us, event | category | flops | bytes accessed | tf_op | source)
XLA Modules:
  0.0 40.1 jit_solution(2981232715747526453)
XLA Ops:
  0.6 38.5 %shard_map.183 = (bf16[64,288]{1,0:T(8,128)(2,1)S(1)}, bf16[64,5568]{1,0:T(8,128)(2,1)S(1)}, f32[32,1,128]{2,1,0:T(1,128)S(1)}, f32[16,4,288]{2,1,0:T(4,128)S(1)}) custom-call(bf16[64,288]{1,0:T(8,128)(2,1)} %state_hbm.1, bf16[64,5568]{1,0:T(8,128)(2,1)} %fields_hbm.1, s32[64]{0:T(128)} %active_hbm.1, f32[58]{0:T(128)} %density_hbm.1, s32[64]{0:T(128)} %span_map_hbm.1, ...), custom_call_target="tpu_custom_call" | custom-call | tf_op jit(solution)/shard_map/pallas_call | solution.py:506
  39.1 1.0 %shard_map.184 = (bf16[64,288]{1,0:T(8,128)(2,1)}, bf16[64,5568]{1,0:T(8,128)(2,1)}, f32[1,24]{1,0:T(1,128)}, f32[16,4,288]{2,1,0:T(4,128)}) custom-call(bf16[64,288]{1,0:T(8,128)(2,1)S(1)} %get-tuple-element.12.tend, bf16[64,5568]{1,0:T(8,128)(2,1)S(1)} %get-tuple-element.13.fresh, f32[32,1,128]{2,1,0:T(1,128)S(1)} %get-tuple-element.14.got, ...), custom_call_target="tpu_custom_call" | custom-call | tf_op jit(solution)/shard_map/pallas_call | solution.py:592

commit v6 on v5

--- a/solution.py
+++ b/solution.py
@@ -436,23 +436,22 @@
 
     @pl.when(parity == 1)
     def _():
-        for n, slot in enumerate((from_lower, from_upper)):
-            for p in range(2):
+        for p in (1, 0):
+            for n, slot in enumerate((from_lower, from_upper)):
                 pltpu.make_async_copy(slot.at[p], slot.at[p], relay_recv.at[n, p]).wait()
-        below, above = lax.rem(span + spans - reach, spans), lax.rem(span + reach, spans)
-
-        def pass_up(i):
-            for p in range(2):
-                give(from_lower.at[p, i], below, i + 1, pass_sem, region - 1 + p)
-
-        def pass_on(i, _):
-            pass_up(reach - 1 - i)
-            for p in range(2):
-                give(from_upper.at[p, i], above, spans - reach + 1 + i, pass_sem, region - 1 + p)
-            return _
-
-        lax.fori_loop(0, reach - 1, pass_on, 0)
-        pass_up(0)
+
+            def pass_up(i, p=p):
+                origin = lax.rem(span + spans - reach, spans)
+                give(from_lower.at[p, i], origin, i + 1, pass_sem, region - 1 + p)
+
+            def pass_on(i, _, p=p):
+                pass_up(reach - 1 - i)
+                origin = lax.rem(span + reach, spans)
+                give(from_upper.at[p, i], origin, spans - reach + 1 + i, pass_sem, region - 1 + p)
+                return _
+
+            lax.fori_loop(0, reach - 1, pass_on, 0)
+            pass_up(0)
 
     for k in range(8):
         give_back(k)

time: 40.3 us -> 39.4 us (0.978)
  the two profiles are of different devices: /device:TPU:1 before, /device:TPU:6 now
where the time goes in v6:
time: 39.4 us; the launch traced here: 39.3 us
  Pallas kernels  38.6 us (98%)
  between operations  0.64 us (2%)
    pallas_call x1, Pallas kernels, crm_call(): pl.pallas_call(functools.partial(crm_kernel, shape), out_shape=(jax.Shape...  37.7 us
    pallas_call x1, Pallas kernels, finish(): pl.pallas_call(finish_kernel, out_shape=tuple(shapes), in_specs=[vmem] *...  0.96 us

profile of v6, /device:TPU:6, one launch (start us, length us, event | category | flops | bytes accessed | tf_op | source)
XLA Modules:
  0.0 39.3 jit_solution(13962606454281094874)
XLA Ops:
  0.6 37.7 %shard_map.183 = (bf16[64,288]{1,0:T(8,128)(2,1)S(1)}, bf16[64,5568]{1,0:T(8,128)(2,1)S(1)}, f32[32,1,128]{2,1,0:T(1,128)S(1)}, f32[16,4,288]{2,1,0:T(4,128)S(1)}) custom-call(bf16[64,288]{1,0:T(8,128)(2,1)} %state_hbm.1, bf16[64,5568]{1,0:T(8,128)(2,1)} %fields_hbm.1, s32[64]{0:T(128)} %active_hbm.1, f32[58]{0:T(128)} %density_hbm.1, s32[64]{0:T(128)} %span_map_hbm.1, ...), custom_call_target="tpu_custom_call" | custom-call | tf_op jit(solution)/shard_map/pallas_call | solution.py:505
  38.3 1.0 %shard_map.184 = (bf16[64,288]{1,0:T(8,128)(2,1)}, bf16[64,5568]{1,0:T(8,128)(2,1)}, f32[1,24]{1,0:T(1,128)}, f32[16,4,288]{2,1,0:T(4,128)}) custom-call(bf16[64,288]{1,0:T(8,128)(2,1)S(1)} %get-tuple-element.12.tend, bf16[64,5568]{1,0:T(8,128)(2,1)S(1)} %get-tuple-element.13.fresh, f32[32,1,128]{2,1,0:T(1,128)S(1)} %get-tuple-element.14.got, ...), custom_call_target="tpu_custom_call" | custom-call | tf_op jit(solution)/shard_map/pallas_call | solution.py:591

commit v7 on v6

--- a/solution.py
+++ b/solution.py
@@ -137,6 +137,8 @@
             pl.semaphore_signal(barrier, inc=1, device_id=along(offset), device_id_type=MESH)
         return _
 
+    lax.fori_loop(0, reach, greet, 0)
+
     def greet_lead(i, _):
         for offset in (reach - i, spans - reach + i):
             pl.semaphore_signal(barrier, inc=1, device_id=along(offset, lead), device_id_type=MESH)
@@ -153,7 +155,6 @@
                 barrier, inc=1, device_id=along(offset, region - 1), device_id_type=MESH
             )
 
-    lax.fori_loop(0, reach, greet, 0)
     for other in (left_device, next_device):
         pl.semaphore_signal(barrier, inc=1, device_id=other, device_id_type=MESH)
 

time: 39.4 us -> 39.5 us (level)
  no operation moved by 1% of the time
where the time goes in v7:
time: 39.5 us; the launch traced here: 39.4 us
  Pallas kernels  38.7 us (98%)
  between operations  0.64 us (2%)
    pallas_call x1, Pallas kernels, crm_call(): pl.pallas_call(functools.partial(crm_kernel, shape), out_shape=(jax.Shape...  37.7 us
    pallas_call x1, Pallas kernels, finish(): pl.pallas_call(finish_kernel, out_shape=tuple(shapes), in_specs=[vmem] *...  0.96 us

profile of v7, /device:TPU:6, one launch (start us, length us, event | category | flops | bytes accessed | tf_op | source)
XLA Modules:
  0.0 39.4 jit_solution(17993652554284444626)
XLA Ops:
  0.6 37.7 %shard_map.183 = (bf16[64,288]{1,0:T(8,128)(2,1)S(1)}, bf16[64,5568]{1,0:T(8,128)(2,1)S(1)}, f32[32,1,128]{2,1,0:T(1,128)S(1)}, f32[16,4,288]{2,1,0:T(4,128)S(1)}) custom-call(bf16[64,288]{1,0:T(8,128)(2,1)} %state_hbm.1, bf16[64,5568]{1,0:T(8,128)(2,1)} %fields_hbm.1, s32[64]{0:T(128)} %active_hbm.1, f32[58]{0:T(128)} %density_hbm.1, s32[64]{0:T(128)} %span_map_hbm.1, ...), custom_call_target="tpu_custom_call" | custom-call | tf_op jit(solution)/shard_map/pallas_call | solution.py:506
  38.4 1.0 %shard_map.184 = (bf16[64,288]{1,0:T(8,128)(2,1)}, bf16[64,5568]{1,0:T(8,128)(2,1)}, f32[1,24]{1,0:T(1,128)}, f32[16,4,288]{2,1,0:T(4,128)}) custom-call(bf16[64,288]{1,0:T(8,128)(2,1)S(1)} %get-tuple-element.12.tend, bf16[64,5568]{1,0:T(8,128)(2,1)S(1)} %get-tuple-element.13.fresh, f32[32,1,128]{2,1,0:T(1,128)S(1)} %get-tuple-element.14.got, ...), custom_call_target="tpu_custom_call" | custom-call | tf_op jit(solution)/shard_map/pallas_call | solution.py:592
